TPU v7x, 256 devices: a whole 4x4x8 slice. The times are simulated.
256 devices in a mesh: row: 8 (over x, z_lo), col: 32 (over z_hi, y, core).
Axes of the slice: x: 4, y: 4, z: 8 (z_hi: 4, z_lo: 2; z = z_hi * 2 + z_lo), core: 2. Of those that a mesh axis runs over, the one named last changes fastest.
Arguments:
- level_set: float32 [12800, 51200], P('row', 'col'), may hold values from -48 to 48
- dose_map: float32 [5120, 20480], P(('row', 'col')), may hold values from 0.6 to 1.6
Outputs:
- exposure: float32 [5120, 20480], P(('row', 'col'))
All inputs are finite; a program needn't handle non-finite values.
Results may differ from a plain program's by a relative error of at most 0.000075.
Values sent between devices are 32-bit elements; how exact they have to be, the bound alone decides.
A program may use at most 128 MiB of HBM per device.

v0:
```python
import math

import jax
import jax.numpy as jnp
from jax import lax
from jax.sharding import PartitionSpec as P

edge_width = 2.0
raw_taps = [math.exp(-0.5 * (offset - 4) ** 2) for offset in range(9)]
blur_taps = [raw_value / sum(raw_taps) for raw_value in raw_taps]


def extended(block, sides, width):
    for axis, dim in sides:
        count = lax.axis_size(axis)
        forward = [(i, i + 1) for i in range(count - 1)]
        backward = [(target, source) for source, target in forward]
        low = lax.ppermute(
            lax.slice_in_dim(block, block.shape[dim] - width, None, axis=dim), axis, forward
        )
        high = lax.ppermute(lax.slice_in_dim(block, 0, width, axis=dim), axis, backward)
        block = jnp.concatenate([low, block, high], axis=dim)
    return block


def tent_table(block_rows):
    centre = 2.5 * jnp.arange(block_rows, dtype=jnp.float32) + 0.75
    places = jnp.arange(block_rows * 5 // 2 + 2, dtype=jnp.float32) - 1.0
    distance = jnp.abs(places[None, :] - centre[:, None])
    return jnp.maximum(0.0, 1.0 - distance / 2.5) / 2.5


def resample_cols(field, tent):
    block_rows = tent.shape[0]
    window_len = tent.shape[1] - 2
    block_count = (field.shape[1] - 2) // window_len
    row_count = field.shape[0]
    leading = field[:, : block_count * window_len].reshape(row_count, block_count, window_len)
    trailing = field[:, 2 : block_count * window_len + 2].reshape(
        row_count, block_count, window_len
    )[:, :, window_len - 2 :]
    windows = jnp.concatenate([leading, trailing], axis=2)
    result = jnp.einsum("rbq,jq->rbj", windows, tent, precision=lax.Precision.HIGHEST)
    return result.reshape(row_count, block_count * block_rows)


def resample_rows(field, tent):
    block_rows = tent.shape[0]
    window_len = tent.shape[1] - 2
    block_count = (field.shape[0] - 2) // window_len
    col_count = field.shape[1]
    leading = field[: block_count * window_len].reshape(block_count, window_len, col_count)
    trailing = field[2 : block_count * window_len + 2].reshape(block_count, window_len, col_count)[
        :, window_len - 2 :
    ]
    windows = jnp.concatenate([leading, trailing], axis=1)
    result = jnp.einsum("jq,bqc->bjc", tent, windows, precision=lax.Precision.HIGHEST)
    return result.reshape(block_count * block_rows, col_count)


def blur_rows(padded):
    length = padded.shape[0] - 8
    summed = blur_taps[0] * padded[0:length]
    for offset in range(1, 9):
        summed = summed + blur_taps[offset] * padded[offset : offset + length]
    return summed


def blur_cols(field):
    length = field.shape[-1]
    padded = jnp.pad(field, [(0, 0)] * (field.ndim - 1) + [(4, 4)])
    summed = blur_taps[0] * padded[..., 0:length]
    for offset in range(1, 9):
        summed = summed + blur_taps[offset] * padded[..., offset : offset + length]
    return summed


def local(level_set, dose_map):
    fine_side = level_set.shape[0]
    tile_side = fine_side * 2 // 5
    tent = tent_table(math.gcd(tile_side, 128))
    padded = extended(level_set, (("row", 0), ("col", 1)), 1)
    colres = resample_cols(padded, tent)
    coarse = resample_rows(colres, tent)
    cover = jax.nn.sigmoid(coarse / edge_width)
    cover_pad = extended(cover, (("row", 0),), 4)
    rowblur = blur_rows(cover_pad)
    stripes = lax.all_to_all(rowblur, "col", split_axis=0, concat_axis=1, tiled=True)
    blurred = blur_cols(stripes)
    return dose_map * blurred


def solution(mesh):
    return jax.shard_map(
        local,
        mesh=mesh,
        in_specs=(P("row", "col"), P(("row", "col"), None)),
        out_specs=P(("row", "col"), None),
        check_vma=False,
    )
```

profile of v0, /device:TPU:32, one launch (start us, length us, event | category | flops | bytes accessed | tf_op | source)
XLA Modules:
  0.0 202.8 jit_solution(9636551615122422893)
XLA Ops:
  0.0 0.8 fusion.58
  0.8 2.9 %collective-permute-start = (f32[1,1600]{1,0:T(1,128)S(1)}, f32[1,1600]{1,0:T(1,128)S(1)}, u32[]{:S(2)}, u32[]{:S(2)}) collective-permute-start(f32[1,1600]{1,0:T(1,128)S(1)} %get-tuple-element.10), channel_id=1, source_target_pairs={{0,32},{32,64},{64,96},{96,128},{128,160},{160,192},{192,224},{1,3... | collective-permute-start | bytes 19208 | tf_op jit(solution)/shard_map/ppermute | solution.py:18
  3.8 2.9 %collective-permute-start.1 = (f32[1,1600]{1,0:T(1,128)S(1)}, f32[1,1600]{1,0:T(1,128)S(1)}, u32[]{:S(2)}, u32[]{:S(2)}) collective-permute-start(f32[1,1600]{1,0:T(1,128)S(1)} %get-tuple-element.9), channel_id=1, source_target_pairs={{32,0},{64,32},{96,64},{128,96},{160,128},{192,160},{224,192},{33,... | collective-permute-start | bytes 19208 | tf_op jit(solution)/shard_map/ppermute | solution.py:21
  6.7 13.2 %copy.22 = f32[1600,1600]{0,1:T(8,128)} copy(f32[1600,1600]{1,0:T(8,128)} %param.2) | data formatting | bytes 20480000 | tf_op args[0]
  19.9 0.3 copy.21
  20.2 0.3 copy.23
  20.5 13.8 %concatenate.29 = f32[1602,1600]{0,1:T(8,128)} concatenate(f32[1,1600]{0,1:T(8,128)S(1)} %copy.21, f32[1600,1600]{0,1:T(8,128)} %copy.22, f32[1,1600]{0,1:T(8,128)S(1)} %copy.23), dimensions={0} | concatenate | bytes 20505600 | tf_op jit(solution)/shard_map/concatenate | solution.py:22
  34.3 0.8 fusion.57
  35.2 1.3 collective-permute-start.2
  36.5 1.3 collective-permute-start.3
  37.8 3.6 %collective-permute-done.3 = f32[1602,1]{0,1:T(1,128)S(1)} collective-permute-done((f32[1602,1]{0,1:T(1,128)S(1)}, f32[1602,1]{0,1:T(1,128)S(1)}, u32[]{:S(2)}, u32[]{:S(2)}) %collective-permute-start.3) | collective-permute-done | bytes 6440 | tf_op jit(solution)/shard_map/ppermute | solution.py:21
  41.3 11.4 %pad_maximum_fusion.1 = (f32[1602,1600]{0,1:T(8,128)S(1)}, f32[1602,1600]{0,1:T(8,128)S(1)}) fusion(f32[1602,1600]{0,1:T(8,128)} %concatenate.29, f32[1602,1]{0,1:T(1,128)S(1)} %collective-permute-done.2, f32[1602,1]{0,1:T(1,128)S(1)} %collective-permute-done.3), kind=kLoop, calls=%fused_computation.5 | loop fusion | flops 5126400 | bytes 30771216 | tf_op jit(solution)/shard_map/concatenate | solution.py:22
  52.8 21.2 %fusion = f32[1602,5,128]{2,0,1:T(8,128)S(1)} fusion(f32[1602,5,2]{0,2,1:T(2,128)S(1)} %slice.127, f32[1602,5,320]{0,2,1:T(8,128)S(1)} %bitcast.14, f32[128]{0:T(128)S(1)} %multiply_add_fusion, f32[322]{0:T(512)S(1)} %iota_add_fusion), kind=kOutput, calls=%fused_computation | convolution fusion | flops 3964508416 | bytes 14419800 | tf_op jit(solution)/shard_map/rbq,jq->rbj/dot_general | solution.py:43
  74.0 2.6 %fusion.59 = (f32[1600,5,128]{2,0,1:T(8,128)}, f32[1600,5,128]{2,0,1:T(8,128)S(1)}) fusion(f32[1602,5,128]{2,0,1:T(8,128)S(1)} %fusion), kind=kLoop, calls=%fused_computation.77 | loop fusion | bytes 16384000 | tf_op jit(solution)/shard_map/slice | solution.py:52
  76.6 10.1 %copy.25 = f32[1600,5,128]{2,1,0:T(8,128)} copy(f32[1600,5,128]{2,0,1:T(8,128)S(1)} %get-tuple-element.12) | data formatting | bytes 8192000 | tf_op jit(solution)/shard_map/slice | solution.py:53
  86.7 6.8 %reshape.39 = f32[5,320,640]{2,1,0:T(8,128)} reshape(f32[1600,5,128]{2,1,0:T(8,128)} %copy.25) | data formatting | bytes 8192000 | tf_op jit(solution)/shard_map/reshape | solution.py:53
  93.5 0.9 slice.130
  94.4 9.8 %copy.24 = f32[1600,5,128]{2,1,0:T(8,128)} copy(f32[1600,5,128]{2,0,1:T(8,128)} %get-tuple-element.11) | data formatting | bytes 8192000 | tf_op jit(solution)/shard_map/slice | solution.py:52
  104.2 6.8 %reshape.38 = f32[5,320,640]{2,1,0:T(8,128)} reshape(f32[1600,5,128]{2,1,0:T(8,128)} %copy.24) | data formatting | bytes 8192000 | tf_op jit(solution)/shard_map/reshape | solution.py:52
  111.1 5.9 %add_divide_fusion = f32[5,640,128]{1,2,0:T(8,128)S(1)} fusion(f32[5,2,640]{2,1,0:T(2,128)S(1)} %slice.130, f32[5,320,640]{2,1,0:T(8,128)} %reshape.38, f32[128]{0:T(128)S(1)} %multiply_add_fusion, f32[322]{0:T(512)S(1)} %iota_add_fusion), kind=kOutput, calls=%fused_computation.51 | convolution fusion | flops 1585610496 | bytes 5761800 | tf_op jit(solution)/shard_map/jq,bqc->bjc/dot_general | solution.py:57
  117.0 3.8 %collective-permute-start.4 = (f32[4,640]{1,0:T(4,128)S(1)}, f32[4,640]{1,0:T(4,128)S(1)}, u32[]{:S(2)}, u32[]{:S(2)}) collective-permute-start(f32[4,640]{1,0:T(4,128)S(1)} %get-tuple-element.13), channel_id=1, source_target_pairs={{0,32},{32,64},{64,96},{96,128},{128,160},{160,192},{192,224},{1,3... | collective-permute-start | bytes 30728 | tf_op jit(solution)/shard_map/ppermute | solution.py:18
  120.9 2.0 collective-permute-start.5
  122.9 4.5 %collective-permute-done.5 = f32[4,640]{1,0:T(4,128)S(1)} collective-permute-done((f32[4,640]{1,0:T(4,128)S(1)}, f32[4,640]{1,0:T(4,128)S(1)}, u32[]{:S(2)}, u32[]{:S(2)}) %collective-permute-start.5) | collective-permute-done | bytes 10272 | tf_op jit(solution)/shard_map/ppermute | solution.py:21
  127.3 3.6 %fusion.16 = f32[640,640]{1,0:T(8,128)} fusion(f32[4,640]{1,0:T(4,128)S(1)} %collective-permute-done.5, f32[4,640]{1,0:T(4,128)S(1)} %collective-permute-done.4, f32[640,640]{1,0:T(8,128)S(1)} %bitcast.20), kind=kLoop, calls=%fused_computation.28 | loop fusion | flops 10240000 | bytes 3297280 | tf_op jit(solution)/shard_map/add | solution.py:65
  130.9 1.5 all_to_all.14
  132.4 63.2 %all_to_all.19 = f32[32,20,640]{2,1,0:T(8,128)S(1)} all-to-all(f32[32,20,640]{2,1,0:T(8,128)S(1)} %all_to_all.14), channel_id=1, replica_groups=mesh['row'=8,'col'=32] {'col'}, dimensions={0} | all-to-all | bytes 3276800 | tf_op jit(solution)/shard_map/all_to_all | solution.py:88
  195.5 0.3 copy.26
  195.9 0.2 pad.25
  196.1 0.0 copy-start
  196.1 1.1 copy.27
  197.2 0.4 copy-done
  197.6 5.1 %add_multiply_fusion = f32[20,20480]{1,0:T(8,128)} fusion(f32[20,20480]{1,0:T(8,128)S(1)} %copy-done, f32[20,20480]{1,0:T(8,128)S(1)} %bitcast.17), kind=kLoop, calls=%fused_computation.16 | loop fusion | flops 7372800 | bytes 4915200 | tf_op jit(solution)/shard_map/mul | solution.py:90
  (8 shorter events, 0.1 us)
Async XLA Ops:
  0.8 19.1 %collective-permute-start = (f32[1,1600]{1,0:T(1,128)S(1)}, f32[1,1600]{1,0:T(1,128)S(1)}, u32[]{:S(2)}, u32[]{:S(2)}) collective-permute-start(f32[1,1600]{1,0:T(1,128)S(1)} %get-tuple-element.10), channel_id=1, source_target_pairs={{0,32},{32,64},{64,96},{96,128},{128,160},{160,192},{192,224},{1,3... | collective-permute-start | bytes 19208 | tf_op jit(solution)/shard_map/ppermute | solution.py:18
  3.8 16.4 %collective-permute-start.1 = (f32[1,1600]{1,0:T(1,128)S(1)}, f32[1,1600]{1,0:T(1,128)S(1)}, u32[]{:S(2)}, u32[]{:S(2)}) collective-permute-start(f32[1,1600]{1,0:T(1,128)S(1)} %get-tuple-element.9), channel_id=1, source_target_pairs={{32,0},{64,32},{96,64},{128,96},{160,128},{192,160},{224,192},{33,... | collective-permute-start | bytes 19208 | tf_op jit(solution)/shard_map/ppermute | solution.py:21
  35.2 2.6 %collective-permute-start.2 = (f32[1602,1]{0,1:T(1,128)S(1)}, f32[1602,1]{0,1:T(1,128)S(1)}, u32[]{:S(2)}, u32[]{:S(2)}) collective-permute-start(f32[1602,1]{0,1:T(1,128)S(1)} %get-tuple-element.7), channel_id=1, source_target_pairs={{0,1},{1,2},{2,3},{3,4},{4,5},{5,6},{6,7},{7,8},{8,9},{9,10},{10,1... | collective-permute-start | bytes 19232 | tf_op jit(solution)/shard_map/ppermute | solution.py:18
  36.5 4.9 %collective-permute-start.3 = (f32[1602,1]{0,1:T(1,128)S(1)}, f32[1602,1]{0,1:T(1,128)S(1)}, u32[]{:S(2)}, u32[]{:S(2)}) collective-permute-start(f32[1602,1]{0,1:T(1,128)S(1)} %get-tuple-element.8), channel_id=1, source_target_pairs={{1,0},{2,1},{3,2},{4,3},{5,4},{6,5},{7,6},{8,7},{9,8},{10,9},{11,1... | collective-permute-start | bytes 19232 | tf_op jit(solution)/shard_map/ppermute | solution.py:21
  117.0 5.9 %collective-permute-start.4 = (f32[4,640]{1,0:T(4,128)S(1)}, f32[4,640]{1,0:T(4,128)S(1)}, u32[]{:S(2)}, u32[]{:S(2)}) collective-permute-start(f32[4,640]{1,0:T(4,128)S(1)} %get-tuple-element.13), channel_id=1, source_target_pairs={{0,32},{32,64},{64,96},{96,128},{128,160},{160,192},{192,224},{1,3... | collective-permute-start | bytes 30728 | tf_op jit(solution)/shard_map/ppermute | solution.py:18
  120.9 6.5 %collective-permute-start.5 = (f32[4,640]{1,0:T(4,128)S(1)}, f32[4,640]{1,0:T(4,128)S(1)}, u32[]{:S(2)}, u32[]{:S(2)}) collective-permute-start(f32[4,640]{1,0:T(4,128)S(1)} %get-tuple-element.14), channel_id=1, source_target_pairs={{32,0},{64,32},{96,64},{128,96},{160,128},{192,160},{224,192},{33,... | collective-permute-start | bytes 30728 | tf_op jit(solution)/shard_map/ppermute | solution.py:21
  196.1 1.5 copy-start
where the time goes:
time: 204 us; the launch traced here: 203 us
  local copies, waits for them, and re-layouts  69.9 us (34%)
  blocking collectives  63.2 us (31%)
  matrix products  27.1 us (13%)
  other arithmetic  20.2 us (10%)
  starting transfers between devices  14.3 us (7%)
  waiting for transfers between devices  8.02 us (4%)
    all_to_all x1, blocking collectives, local(): lax.all_to_all(rowblur, 'col', split_axis=0, concat_axis=1, tiled=True)  63.2 us
    dot_general x1, matrix products, resample_cols(): jnp.einsum('rbq,jq->rbj', windows, tent, precision=lax.Precision.HIGHEST)  21.2 us
    unnamed x5, local copies, waits for them, and re-layouts  14.9 us
    concatenate x1, local copies, waits for them, and re-layouts, extended(): block = jnp.concatenate([low, block, high], axis=dim)  13.8 us
    slice x2, local copies, waits for them, and re-layouts, resample_rows(): field[:block_count * window_len].reshape(block_count, window_len, col_count)  12.4 us
    concatenate x1, other arithmetic, extended(): block = jnp.concatenate([low, block, high], axis=dim)  11.4 us
    slice x2, local copies, waits for them, and re-layouts, resample_rows(): field[2:block_count * window_len + 2]  11.1 us
    ppermute x3, starting transfers between devices, extended(): lax.ppermute(lax.slice_in_dim(block, block.shape[dim] - width, None, axis...  8.08 us
  transfers between devices with their start and end apart: 6, of which 2 were waited for; matrix products, arithmetic and copies ran while one was open for 7% of the time, Pallas kernels for 0%

commit v1 on v0

v1 whole, which is shorter than its diff:
```python
import functools
import math

import jax
import jax.numpy as jnp
from jax import lax
from jax.experimental import pallas as pl
from jax.experimental.pallas import tpu as pltpu
from jax.sharding import PartitionSpec as P

F32, BF16 = jnp.float32, jnp.bfloat16
MESH = pl.DeviceIdType.MESH
RAW_TAPS = [math.exp(-0.5 * k * k) for k in range(5)]
TAPS = [t / (RAW_TAPS[0] + 2.0 * sum(RAW_TAPS[1:])) for t in RAW_TAPS]

FINE, TILE, STRIPE = 1600, 640, 20
TOP = 24
XROWS = TOP + FINE + 24
CROWS = 656
CHUNK = 208
LANES = 1664
BASES = (0, 256, 512, 896, 1152)
SLOT = 100
PART_A = 60


def row_groups(x_ref, group, out_ref, out_row):
    start = TOP - 20 + 40 * group
    for tile in range(LANES // 128):
        a = [x_ref[tile, pl.ds(start + s, 8, stride=5), :] for s in range(-1, 6)]
        even = 3.0 * a[0] + 7.0 * a[1] + 9.0 * a[2] + 5.0 * a[3] + a[4]
        odd = a[2] + 5.0 * a[3] + 9.0 * a[4] + 7.0 * a[5] + 3.0 * a[6]
        out_ref[tile, pl.ds(out_row, 8, stride=2), :] = even
        out_ref[tile, pl.ds(out_row + 1, 8, stride=2), :] = odd


def col_tile(rr_ref, count, w_ref, tile):
    first = BASES[tile] // 128
    rows = jnp.concatenate([rr_ref[first + t, 0:count, :] for t in range(4)], axis=1)
    hi = rows.astype(BF16)
    rest = rows - hi.astype(F32)
    mid = rest.astype(BF16)
    low = (rest - mid.astype(F32)).astype(BF16)
    w = w_ref[tile]
    dot = functools.partial(jnp.dot, preferred_element_type=F32)
    return dot(hi, w) + dot(mid, w) + dot(low, w)


def coverage(total):
    return 1.0 / (1.0 + jnp.exp(total * (-1.0 / 1250.0)))


def blur_block(cov_ref, d, tile):
    first = STRIPE * d + 4
    taps = [cov_ref[tile, pl.ds(first + k, STRIPE), :] for k in range(9)]
    total = TAPS[0] * taps[4]
    for k in range(1, 5):
        total = total + TAPS[k] * (taps[4 - k] + taps[4 + k])
    return total


def piece_a(cov_ref, send_ref, d):
    for t in range(3):
        send_ref[d, STRIPE * t : STRIPE * t + STRIPE, :] = blur_block(cov_ref, d, t + 1)


def piece_b(cov_ref, send_ref, d):
    for t in range(2):
        send_ref[d, PART_A + STRIPE * t : PART_A + STRIPE * t + STRIPE, :] = blur_block(cov_ref, d, 4 * t)


def tile_kernel(
    n_row, n_col, x_hbm, got_ref,
    x_in, x_ref, w_ref, rr_ref, cov_ref, send_ref, strip_ref, halo_out, halo_in,
    load_sem, row_send, row_recv, col_send, col_recv, send_sem, recv_sem, own_sem,
):
    row, col = lax.axis_index("row"), lax.axis_index("col")
    z, y, core = col // 8, lax.rem(col // 2, 4), lax.rem(col, 2)
    up, down, left, right = row > 0, row < n_row - 1, col > 0, col < n_col - 1

    def load(part):
        rows = pl.ds(400 * part, 400)
        return pltpu.make_async_copy(x_hbm.at[rows], x_in.at[rows], load_sem.at[part])

    for part in range(4):
        load(part).start()

    barrier = pltpu.get_barrier_semaphore()

    @pl.loop(1, n_col)
    def _(k):
        pl.semaphore_signal(barrier, 1, device_id=(row, lax.rem(col + k, n_col)), device_id_type=MESH)

    for there, other in ((up, row - 1), (down, row + 1)):
        @pl.when(there)
        def _(other=other):
            pl.semaphore_signal(barrier, 1, device_id=(other, col), device_id_type=MESH)

    k_at = lax.broadcasted_iota(jnp.int32, (512, 128), 0)
    n_at = lax.broadcasted_iota(jnp.int32, (512, 128), 1)
    for tile in range(5):
        far = jnp.abs(4 * k_at - 10 * n_at + (4 * BASES[tile] - 1280 * tile - 3))
        w_ref[tile] = jnp.maximum(10 - far, 0).astype(F32).astype(BF16)
    x_ref[12, TOP : TOP + FINE, 64:128] = jnp.zeros((FINE, 64), F32)
    x_ref[:, 0:8, :] = jnp.zeros((13, 8, 128), F32)
    x_ref[:, XROWS - 8 : XROWS, :] = jnp.zeros((13, 8, 128), F32)
    strip_ref[:, CROWS:768, :] = jnp.zeros((2, 768 - CROWS, 128), F32)
    halo_in[0, 8:128, :] = jnp.zeros((120, 768), F32)
    halo_in[1, 0:120, :] = jnp.zeros((120, 768), F32)

    @pl.when(jnp.logical_not(up))
    def _():
        x_ref[:, 8:24, :] = jnp.zeros((13, 16, 128), F32)

    @pl.when(jnp.logical_not(down))
    def _():
        x_ref[:, XROWS - 24 : XROWS - 8, :] = jnp.zeros((13, 16, 128), F32)

    @pl.when(jnp.logical_not(left))
    def _():
        halo_in[0, 0:8, :] = jnp.zeros((8, 768), F32)

    @pl.when(jnp.logical_not(right))
    def _():
        halo_in[1, 120:128, :] = jnp.zeros((8, 768), F32)

    for part in range(4):
        load(part).wait()

        @pl.loop(0, 10)
        def _(g, part=part):
            start = pl.multiple_of(400 * part + 40 * g, 8)
            for tile in range(12):
                x_ref[tile, pl.ds(TOP + start, 40), :] = x_in[pl.ds(start, 40), 128 * tile : 128 * tile + 128]
            x_ref[12, pl.ds(TOP + start, 40), 0:64] = x_in[pl.ds(start, 40), 1536:1600]

    @pl.loop(0, 3)
    def _(chunk):
        @pl.loop(0, 13)
        def _(g):
            row_groups(x_ref, 1 + 13 * chunk + g, rr_ref, 16 * g)

        at = pl.ds(pl.multiple_of(16 + CHUNK * chunk, 16), CHUNK)
        strip_ref[0, at, :] = rr_ref[0]
        strip_ref[1, at, :] = rr_ref[12]
        for tile in range(5):
            total = col_tile(rr_ref, CHUNK, w_ref, tile)
            cov_ref[tile, at, :] = total if tile in (0, 4) else coverage(total)

    @pl.loop(1, n_col - 1)
    def _(d):
        piece_a(cov_ref, send_ref, d)

    pl.semaphore_wait(barrier, n_col - 1 + up.astype(jnp.int32) + down.astype(jnp.int32))

    def row_halo(i):
        if i == 0:
            return pltpu.make_async_remote_copy(
                x_ref.at[:, pl.ds(TOP + FINE - 16, 16)], x_ref.at[:, pl.ds(TOP - 16, 16)],
                row_send.at[0], row_recv.at[0], device_id=(row + 1, col), device_id_type=MESH)
        return pltpu.make_async_remote_copy(
            x_ref.at[:, pl.ds(TOP, 16)], x_ref.at[:, pl.ds(TOP + FINE, 16)],
            row_send.at[1], row_recv.at[1], device_id=(row - 1, col), device_id_type=MESH)

    def col_halo(i):
        if i == 0:
            return pltpu.make_async_remote_copy(
                halo_out.at[0], halo_in.at[0, pl.ds(0, 8)],
                col_send.at[0], col_recv.at[0], device_id=(row, col + 1), device_id_type=MESH)
        return pltpu.make_async_remote_copy(
            halo_out.at[1], halo_in.at[1, pl.ds(120, 8)],
            col_send.at[1], col_recv.at[1], device_id=(row, col - 1), device_id_type=MESH)

    @pl.when(down)
    def _():
        row_halo(0).start()

    @pl.when(up)
    def _():
        row_halo(1).start()

    def piece(part, d, slot):
        rows = pl.ds(0, PART_A) if part == 0 else pl.ds(PART_A, SLOT - PART_A)
        return pltpu.make_async_remote_copy(
            send_ref.at[d, rows], got_ref.at[slot, rows],
            send_sem.at[part, d], recv_sem.at[part, slot], device_id=(row, d), device_id_type=MESH)

    def target(i):
        far = i < 24
        j = jnp.where(far, i // 3, i - 24)
        dz = jnp.where(far, 1 + lax.rem(2 * lax.rem(i, 3), 3), 0)
        return lax.rem(z + dz, 4) * 8 + lax.rem(y + j // 2, 4) * 2 + lax.rem(core + lax.rem(j, 2), 2)

    def inner(d):
        return jnp.logical_and(d > 0, d < n_col - 1)

    @pl.loop(0, n_col)
    def _(i):
        d = target(i)

        @pl.when(jnp.logical_and(inner(d), i != 24))
        def _():
            piece(0, d, col).start()

    @pl.when(up)
    def _():
        row_halo(0).wait_recv()

    @pl.when(down)
    def _():
        row_halo(1).wait_recv()

    row_groups(x_ref, 0, rr_ref, 0)
    row_groups(x_ref, 40, rr_ref, 16)
    strip_ref[0, 0:16, :] = rr_ref[0, 0:16, :]
    strip_ref[1, 0:16, :] = rr_ref[12, 0:16, :]
    strip_ref[0, CROWS - 16 : CROWS, :] = rr_ref[0, 16:32, :]
    strip_ref[1, CROWS - 16 : CROWS, :] = rr_ref[12, 16:32, :]

    sub = lax.broadcasted_iota(jnp.int32, (8, 768), 0)
    last = jnp.transpose(strip_ref[1])[63:64, :]
    halo_out[0] = jnp.where(sub == 0, 3.0 * last, 0.0)
    first = jnp.transpose(strip_ref[0])[0:1, :]
    halo_out[1] = jnp.where(sub == 7, 3.0 * first, 0.0)

    @pl.when(right)
    def _():
        col_halo(0).start()

    @pl.when(left)
    def _():
        col_halo(1).start()

    def in_window(i0, count):
        j = lax.broadcasted_iota(jnp.int32, (count, 128), 0) + (TILE * row + i0 - 8)
        return jnp.logical_and(j >= 0, j < TILE * n_row)

    for tile in range(5):
        total = col_tile(rr_ref, 32, w_ref, tile)
        for part, i0 in ((total[0:16], 0), (total[16:32], CROWS - 16)):
            if tile not in (0, 4):
                part = jnp.where(in_window(i0, 16), coverage(part), 0.0)
            cov_ref[tile, i0 : i0 + 16, :] = part

    for d in (0, n_col - 1):
        piece_a(cov_ref, send_ref, d)

        @pl.when(col != d)
        def _(d=d):
            piece(0, d, col).start()

    for side, there in ((0, left), (1, right)):
        @pl.when(there)
        def _(side=side):
            col_halo(side).wait_recv()

        extra = jnp.transpose(halo_in[side])
        total = cov_ref[4 * side] + extra[0:CROWS]
        cov_ref[4 * side] = jnp.where(in_window(0, CROWS), coverage(total), 0.0)

    @pl.loop(0, n_col)
    def _(i):
        d = target(i)
        piece_b(cov_ref, send_ref, d)

        @pl.when(i != 24)
        def _():
            piece(1, d, col).start()

    own = pltpu.make_async_copy(send_ref.at[col], got_ref.at[col], own_sem)
    own.start()

    @pl.when(down)
    def _():
        row_halo(0).wait_send()

    @pl.when(up)
    def _():
        row_halo(1).wait_send()

    @pl.when(right)
    def _():
        col_halo(0).wait_send()

    @pl.when(left)
    def _():
        col_halo(1).wait_send()

    own.wait()

    @pl.loop(0, n_col)
    def _(k):
        @pl.when(k != col)
        def _():
            for part in range(2):
                piece(part, k, k).wait_send()
                piece(part, k, k).wait_recv()


def exchange(level_set, n_row, n_col):
    any_space = pl.BlockSpec(memory_space=pl.ANY)
    return pl.pallas_call(
        functools.partial(tile_kernel, n_row, n_col),
        out_shape=jax.ShapeDtypeStruct((n_col, SLOT, 128), F32),
        in_specs=[any_space],
        out_specs=any_space,
        scratch_shapes=[
            pltpu.VMEM((FINE, FINE), F32),
            pltpu.VMEM((13, XROWS, 128), F32),
            pltpu.VMEM((5, 512, 128), BF16),
            pltpu.VMEM((13, CHUNK, 128), F32),
            pltpu.VMEM((5, CROWS, 128), F32),
            pltpu.VMEM((n_col, SLOT, 128), F32),
            pltpu.VMEM((2, 768, 128), F32),
            pltpu.VMEM((2, 8, 768), F32),
            pltpu.VMEM((2, 128, 768), F32),
            pltpu.SemaphoreType.DMA((4,)),
            pltpu.SemaphoreType.DMA((2,)),
            pltpu.SemaphoreType.DMA((2,)),
            pltpu.SemaphoreType.DMA((2,)),
            pltpu.SemaphoreType.DMA((2,)),
            pltpu.SemaphoreType.DMA((2, n_col)),
            pltpu.SemaphoreType.DMA((2, n_col)),
            pltpu.SemaphoreType.DMA,
        ],
        compiler_params=pltpu.CompilerParams(
            collective_id=0, has_side_effects=True, vmem_limit_bytes=48 << 20
        ),
        name="resample_exchange",
    )(level_set)


STEP = 4


def slot_rows(ref, at, tile):
    first = STRIPE * (tile - 1) if 0 < tile < 4 else PART_A + STRIPE * (tile // 4)
    return ref[at, first : first + STRIPE, :]


def finish_kernel(steps, prev_ref, cur_ref, next_ref, dose_ref, out_ref):
    step = pl.program_id(0)
    width = STEP * TILE
    before = jnp.where(step > 0, slot_rows(prev_ref, 0, 4), 0.0)
    after = jnp.where(step < steps - 1, slot_rows(next_ref, 0, 0), 0.0)
    field = jnp.concatenate(
        [before] + [slot_rows(cur_ref, s, t) for s in range(STEP) for t in range(5)] + [after],
        axis=1,
    )
    total = TAPS[0] * field
    for k in range(1, 5):
        total = total + TAPS[k] * (pltpu.roll(field, k, 1) + pltpu.roll(field, width + 256 - k, 1))
    out_ref[...] = dose_ref[...] * total[:, 128 : 128 + width]


def finish(got, dose_map, n_col):
    steps = n_col // STEP
    return pl.pallas_call(
        functools.partial(finish_kernel, steps),
        grid=(steps,),
        out_shape=jax.ShapeDtypeStruct(dose_map.shape, F32),
        in_specs=[
            pl.BlockSpec((1, SLOT, 128), lambda i: (jnp.maximum(STEP * i - 1, 0), 0, 0)),
            pl.BlockSpec((STEP, SLOT, 128), lambda i: (i, 0, 0)),
            pl.BlockSpec((1, SLOT, 128), lambda i: (jnp.minimum(STEP * i + STEP, n_col - 1), 0, 0)),
            pl.BlockSpec((STRIPE, STEP * TILE), lambda i: (0, i)),
        ],
        out_specs=pl.BlockSpec((STRIPE, STEP * TILE), lambda i: (0, i)),
        name="finish",
    )(got, got, got, dose_map)


def solution(mesh):
    n_row, n_col = mesh.shape["row"], mesh.shape["col"]

    def local(level_set, dose_map):
        return finish(exchange(level_set, n_row, n_col), dose_map, n_col)

    return jax.shard_map(
        local,
        mesh=mesh,
        in_specs=(P("row", "col"), P(("row", "col"), None)),
        out_specs=P(("row", "col"), None),
        check_vma=False,
    )
```

time: 204 us -> 72.3 us (0.35)
  the two profiles are of different devices: /device:TPU:32 before, /device:TPU:31 now
where the time goes in v1:
time: 72.3 us; the launch traced here: 72 us
  Pallas kernels  70.8 us (98%)
  local copies, waits for them, and re-layouts  1.19 us (2%)
    pallas_call x1, Pallas kernels, exchange(): pl.pallas_call(functools.partial(tile_kernel, n_row, n_col), out_shape=ja...  62.2 us
    pallas_call x1, Pallas kernels, finish(): pl.pallas_call(functools.partial(finish_kernel, steps), grid=(steps,), ou...  8.65 us

profile of v1, /device:TPU:31, one launch (start us, length us, event | category | flops | bytes accessed | tf_op | source)
XLA Modules:
  0.0 72.0 jit_solution(16044661298786412476)
XLA Ops:
  0.0 62.2 %resample_exchange.1.prev_ref.cur_ref.next_ref = f32[32,100,128]{2,1,0:T(8,128)S(1)} custom-call(f32[1600,1600]{1,0:T(8,128)} %x_hbm.1), custom_call_target="tpu_custom_call" | custom-call | tf_op jit(solution)/shard_map/resample_exchange/pallas_call | solution.py:302
  62.2 0.0 copy-start
  62.2 1.2 %copy-done = f32[32,100,128]{2,1,0:T(8,128)} copy-done((f32[32,100,128]{2,1,0:T(8,128)}, f32[32,100,128]{2,1,0:T(8,128)S(1)}, u32[]{:S(2)}) %copy-start) | copy-done | bytes 1638424
  63.4 8.6 %finish.1 = f32[20,20480]{1,0:T(8,128)} custom-call(f32[32,100,128]{2,1,0:T(8,128)} %copy-done, f32[32,100,128]{2,1,0:T(8,128)} %copy-done, f32[32,100,128]{2,1,0:T(8,128)} %copy-done, f32[20,20480]{1,0:T(8,128)} %dose_ref.1), custom_call_target="tpu_custom_call" | custom-call | tf_op jit(solution)/shard_map/finish/pallas_call | solution.py:358
Async XLA Ops:
  62.2 1.2 %copy-start = (f32[32,100,128]{2,1,0:T(8,128)}, f32[32,100,128]{2,1,0:T(8,128)S(1)}, u32[]{:S(2)}) copy-start(f32[32,100,128]{2,1,0:T(8,128)S(1)} %resample_exchange.1.prev_ref.cur_ref.next_ref) | copy-start | bytes 4915204

commit v2 on v0

v2 whole, which is shorter than its diff:
```python
import functools
import math

import jax
import jax.numpy as jnp
from jax import lax
from jax.experimental import pallas as pl
from jax.experimental.pallas import tpu as pltpu
from jax.sharding import PartitionSpec as P

F32, BF16 = jnp.float32, jnp.bfloat16
MESH = pl.DeviceIdType.MESH
RAW_TAPS = [math.exp(-0.5 * k * k) for k in range(5)]
TAPS = [t / (RAW_TAPS[0] + 2.0 * sum(RAW_TAPS[1:])) for t in RAW_TAPS]

FINE, TILE, STRIPE = 1600, 640, 20
TILES = 13
PART = 464
CHUNK = 176
CROWS = 656
HROWS = 768
BASES = (0, 256, 512, 896, 1152)
SLOT = 100
PART_A = 60


def to_tiles(src_ref, src_at, dst_ref, dst_at, count):
    for tile in range(TILES - 1):
        dst_ref[tile, pl.ds(dst_at, count), :] = src_ref[pl.ds(src_at, count), 128 * tile : 128 * tile + 128]
    dst_ref[12, pl.ds(dst_at, count), 0:64] = src_ref[pl.ds(src_at, count), 1536:1600]


def row_groups(x_ref, start, out_ref, out_row):
    for tile in range(TILES):
        a = [x_ref[tile, pl.ds(start + s, 8, stride=5), :] for s in range(-1, 6)]
        even = 3.0 * a[0] + 7.0 * a[1] + 9.0 * a[2] + 5.0 * a[3] + a[4]
        odd = a[2] + 5.0 * a[3] + 9.0 * a[4] + 7.0 * a[5] + 3.0 * a[6]
        out_ref[tile, pl.ds(out_row, 8, stride=2), :] = even
        out_ref[tile, pl.ds(out_row + 1, 8, stride=2), :] = odd


def dot(a, b):
    return jnp.dot(a, b, preferred_element_type=F32)


def tent_dot(rows, w):
    hi = rows.astype(BF16)
    rest = rows - hi.astype(F32)
    mid = rest.astype(BF16)
    low = (rest - mid.astype(F32)).astype(BF16)
    return dot(hi, w) + dot(mid, w) + dot(low, w)


def col_tile(rr_ref, count, w_ref, tile):
    first = BASES[tile] // 128
    return tent_dot(jnp.concatenate([rr_ref[first + t, 0:count, :] for t in range(4)], axis=1), w_ref[tile])


def coverage(total):
    return 1.0 / (1.0 + jnp.exp(total * (-1.0 / 1250.0)))


def halves(cover):
    hi = cover.astype(BF16)
    return hi, (cover - hi.astype(F32)).astype(BF16)


def col_blur(pieces, g_ref):
    hi = jnp.concatenate([p[0] for p in pieces], axis=1)
    low = jnp.concatenate([p[1] for p in pieces], axis=1)
    return dot(hi, g_ref[0]) + dot(low, g_ref[0]) + dot(hi, g_ref[1])


def row_blur(cb_ref, d, tile):
    first = STRIPE * d + 4
    taps = [cb_ref[tile, pl.ds(first + k, STRIPE), :] for k in range(9)]
    total = TAPS[0] * taps[4]
    for k in range(1, 5):
        total = total + TAPS[k] * (taps[4 - k] + taps[4 + k])
    return total


def piece_a(cb_ref, send_ref, d):
    for t in range(3):
        send_ref[d, STRIPE * t : STRIPE * t + STRIPE, :] = row_blur(cb_ref, d, t + 1)


def piece_b(cb_ref, send_ref, d):
    for t in range(2):
        send_ref[d, PART_A + STRIPE * t : PART_A + STRIPE * t + STRIPE, :] = row_blur(cb_ref, d, 4 * t)


def make_weights(w_ref, we_ref, g_ref):
    def tent(fine_col, coarse_col):
        return jnp.maximum(10 - jnp.abs(4 * fine_col - 10 * coarse_col - 3), 0)

    k = lax.broadcasted_iota(jnp.int32, (512, 128), 0)
    n = lax.broadcasted_iota(jnp.int32, (512, 128), 1)
    for tile in range(5):
        w_ref[tile] = tent(k + BASES[tile], n + 128 * tile).astype(F32).astype(BF16)

    k = lax.broadcasted_iota(jnp.int32, (128, 128), 0)
    n = lax.broadcasted_iota(jnp.int32, (128, 128), 1)
    beyond = jnp.where(n < 4, n + 640, n - 128)
    is_beyond = jnp.logical_or(n < 4, n >= 124)
    halo_col = jnp.where(k < 16, k - 16, k + 1584)
    is_halo = k < 32
    zero = jnp.zeros((128, 128), BF16)
    for part, (fine, use) in enumerate(((k, k >= 0), (k + 1536, k < 64), (halo_col, is_halo))):
        for out, (coarse, ok) in enumerate(((n, use), (n + 512, use), (beyond, jnp.logical_and(use, is_beyond)))):
            rows, cols = pl.ds(128 * part, 128), pl.ds(128 * out, 128)
            if part < 2 and out < 2:
                we_ref[rows, cols] = zero
            else:
                we_ref[rows, cols] = jnp.where(ok, tent(fine, coarse), 0).astype(F32).astype(BF16)

    k = lax.broadcasted_iota(jnp.int32, (384, 128), 0)
    n = lax.broadcasted_iota(jnp.int32, (384, 128), 1)
    off = jnp.abs(k - n - 128)
    g = jnp.zeros((384, 128), F32)
    for step in range(5):
        g = jnp.where(off == step, TAPS[step], g)
    hi, low = halves(g)
    g_ref[0] = hi
    g_ref[1] = low


def tile_kernel(
    n_row, n_col, x_hbm, dose_hbm, out_hbm,
    x_in, x_top, x_bot, x_ref, top_ref, bot_ref, w_ref, we_ref, g_ref, rr_ref, sum_ref, cov_ref, cb_ref,
    strip_ref, halo_out, halo_in, send_ref, got_ref, dose_ref, out_ref,
    load_sem, edge_sem, dose_sem, row_send, row_recv, col_send, col_recv, send_sem, recv_sem, own_sem, out_sem,
):
    row, col = lax.axis_index("row"), lax.axis_index("col")
    z, y, core = col // 8, lax.rem(col // 2, 4), lax.rem(col, 2)
    up, down, left, right = row > 0, row < n_row - 1, col > 0, col < n_col - 1

    def chunk_at(step):
        return lax.rem(z + jnp.where(step == 0, 2, jnp.where(step == 1, 1, jnp.where(step == 2, 3, 0))), 4)

    def load_start(c):
        return pl.multiple_of(jnp.clip(400 * c - 24, 0, FINE - PART), 8)

    def load(c):
        return pltpu.make_async_copy(x_hbm.at[pl.ds(load_start(c), PART)], x_in.at[c], load_sem.at[c])

    load(chunk_at(0)).start()
    edges = [
        pltpu.make_async_copy(x_hbm.at[pl.ds(0, 24)], x_top, edge_sem.at[0]),
        pltpu.make_async_copy(x_hbm.at[pl.ds(FINE - 24, 24)], x_bot, edge_sem.at[1]),
    ]
    for edge in edges:
        edge.start()
    for step in range(1, 4):
        load(chunk_at(step)).start()
    dose = pltpu.make_async_copy(dose_hbm, dose_ref, dose_sem)
    dose.start()

    top_ref[:, 0:8, :] = jnp.zeros((TILES, 8, 128), F32)
    bot_ref[:, 40:48, :] = jnp.zeros((TILES, 8, 128), F32)
    halo_in[32:128, :] = jnp.zeros((96, HROWS), F32)

    @pl.when(jnp.logical_not(up))
    def _():
        top_ref[:, 8:24, :] = jnp.zeros((TILES, 16, 128), F32)

    @pl.when(jnp.logical_not(down))
    def _():
        bot_ref[:, 24:40, :] = jnp.zeros((TILES, 16, 128), F32)

    @pl.when(jnp.logical_not(left))
    def _():
        halo_in[0:16, :] = jnp.zeros((16, HROWS), F32)

    @pl.when(jnp.logical_not(right))
    def _():
        halo_in[16:32, :] = jnp.zeros((16, HROWS), F32)

    barrier = pltpu.get_barrier_semaphore()

    @pl.loop(1, n_col)
    def _(k):
        pl.semaphore_signal(barrier, 1, device_id=(row, lax.rem(col + k, n_col)), device_id_type=MESH)

    for there, other in ((up, row - 1), (down, row + 1)):
        @pl.when(there)
        def _(other=other):
            pl.semaphore_signal(barrier, 1, device_id=(other, col), device_id_type=MESH)

    make_weights(w_ref, we_ref, g_ref)
    x_ref[12, :, 64:128] = jnp.zeros((PART, 64), F32)
    top_ref[12, 24:48, 64:128] = jnp.zeros((24, 64), F32)
    bot_ref[12, 0:24, 64:128] = jnp.zeros((24, 64), F32)
    strip_ref[0:2, CROWS:HROWS, :] = jnp.zeros((2, HROWS - CROWS, 128), F32)

    def row_halo(i):
        if i == 0:
            return pltpu.make_async_remote_copy(
                bot_ref.at[:, pl.ds(8, 16)], top_ref.at[:, pl.ds(8, 16)],
                row_send.at[0], row_recv.at[0], device_id=(row + 1, col), device_id_type=MESH)
        return pltpu.make_async_remote_copy(
            top_ref.at[:, pl.ds(24, 16)], bot_ref.at[:, pl.ds(24, 16)],
            row_send.at[1], row_recv.at[1], device_id=(row - 1, col), device_id_type=MESH)

    def col_halo(i):
        if i == 0:
            return pltpu.make_async_remote_copy(
                halo_out.at[0], halo_in.at[pl.ds(0, 16)],
                col_send.at[0], col_recv.at[0], device_id=(row, col + 1), device_id_type=MESH)
        return pltpu.make_async_remote_copy(
            halo_out.at[1], halo_in.at[pl.ds(16, 16)],
            col_send.at[1], col_recv.at[1], device_id=(row, col - 1), device_id_type=MESH)

    def piece(part, d, slot):
        rows = pl.ds(0, PART_A) if part == 0 else pl.ds(PART_A, SLOT - PART_A)
        return pltpu.make_async_remote_copy(
            send_ref.at[d, rows], got_ref.at[slot, rows],
            send_sem.at[part, d], recv_sem.at[part, slot], device_id=(row, d), device_id_type=MESH)

    def in_chunk(c, s):
        return 8 * c + lax.rem(y + s // 2, 4) * 2 + lax.rem(core + lax.rem(s, 2), 2)

    def resample(c):
        load(c).wait()
        base = load_start(c)

        @pl.loop(0, PART // 8)
        def _(g):
            at = pl.multiple_of(8 * g, 8)
            to_tiles(x_in.at[c], at, x_ref, at, 8)

        first = jnp.clip(10 * c, 1, 29)

        @pl.loop(0, 11)
        def _(g):
            row_groups(x_ref, 40 * (first + g) - 20 - base, rr_ref, 16 * g)

        at = pl.ds(16 * first, CHUNK)
        strip_ref[0, at, :] = rr_ref[0]
        strip_ref[1, at, :] = rr_ref[12]
        cover = []
        for tile in range(5):
            total = col_tile(rr_ref, CHUNK, w_ref, tile)
            if tile in (0, 4):
                sum_ref[tile // 4, at, :] = total
            total = coverage(total)
            if tile in (1, 3):
                cov_ref[tile // 2, at, :] = total
            cover.append(halves(total))
        for tile in range(1, 4):
            cb_ref[tile, at, :] = col_blur(cover[tile - 1 : tile + 2], g_ref)

    def send_a(c):
        @pl.loop(0, 8)
        def _(s):
            d = in_chunk(c, s)

            @pl.when(jnp.logical_and(d > 0, d < n_col - 1))
            def _():
                piece_a(cb_ref, send_ref, d)

                @pl.when(d != col)
                def _():
                    piece(0, d, col).start()

    @pl.loop(0, 4)
    def _(step):
        c = chunk_at(step)
        resample(c)

        @pl.when(step == 0)
        def _():
            for edge in edges:
                edge.wait()
            to_tiles(x_top, 0, top_ref, 24, 24)
            to_tiles(x_bot, 0, bot_ref, 0, 24)
            pl.semaphore_wait(barrier, n_col - 1 + up.astype(jnp.int32) + down.astype(jnp.int32))

            @pl.when(down)
            def _():
                row_halo(0).start()

            @pl.when(up)
            def _():
                row_halo(1).start()

        send_a(c)

    @pl.when(up)
    def _():
        row_halo(0).wait_recv()

    @pl.when(down)
    def _():
        row_halo(1).wait_recv()

    row_groups(top_ref, 4, rr_ref, 0)
    row_groups(bot_ref, 4, rr_ref, 16)
    ends = ((slice(0, 16), 0), (slice(16, 32), CROWS - 16))
    for part, i0 in ends:
        strip_ref[0, i0 : i0 + 16, :] = rr_ref[0, part, :]
        strip_ref[1, i0 : i0 + 16, :] = rr_ref[12, part, :]

    halo_out[0] = jnp.transpose(strip_ref[1])[48:64, :]
    halo_out[1] = jnp.transpose(strip_ref[0])[0:16, :]

    @pl.when(right)
    def _():
        col_halo(0).start()

    @pl.when(left)
    def _():
        col_halo(1).start()

    def in_window(i0, count):
        j = lax.broadcasted_iota(jnp.int32, (count, 128), 0) + (TILE * row + i0 - 8)
        return jnp.logical_and(j >= 0, j < TILE * n_row)

    cover = []
    end_rows = jnp.concatenate([in_window(0, 16), in_window(CROWS - 16, 16)], axis=0)
    for tile in range(5):
        total = col_tile(rr_ref, 32, w_ref, tile)
        if tile in (0, 4):
            for part, i0 in ends:
                sum_ref[tile // 4, i0 : i0 + 16, :] = total[part]
        total = jnp.where(end_rows, coverage(total), 0.0)
        if tile in (1, 3):
            for part, i0 in ends:
                cov_ref[tile // 2, i0 : i0 + 16, :] = total[part]
        cover.append(halves(total))
    for tile in range(1, 4):
        total = col_blur(cover[tile - 1 : tile + 2], g_ref)
        for part, i0 in ends:
            cb_ref[tile, i0 : i0 + 16, :] = total[part]

    for d in (0, n_col - 1):
        piece_a(cb_ref, send_ref, d)

        @pl.when(col != d)
        def _(d=d):
            piece(0, d, col).start()

    @pl.when(left)
    def _():
        col_halo(0).wait_recv()

    @pl.when(right)
    def _():
        col_halo(1).wait_recv()

    halo = jnp.transpose(halo_in[...])
    for part in range(HROWS // 128):
        strip_ref[2, 128 * part : 128 * part + 128, :] = halo[128 * part : 128 * part + 128]

    lane = lax.broadcasted_iota(jnp.int32, (CHUNK, 128), 1)

    @pl.loop(0, 4)
    def _(step):
        c = chunk_at(step)
        at = pl.ds(160 * c, CHUNK)
        extra = tent_dot(jnp.concatenate([strip_ref[k, at, :] for k in range(3)], axis=1), we_ref[...])
        inside = in_window(160 * c, CHUNK)
        first = jnp.where(inside, coverage(sum_ref[0, at, :] + extra[:, 0:128]), 0.0)
        last = jnp.where(inside, coverage(sum_ref[1, at, :] + extra[:, 128:256]), 0.0)
        held = jnp.logical_or(jnp.logical_and(right, lane < 4), jnp.logical_and(left, lane >= 124))
        beyond = jnp.where(jnp.logical_and(inside, held), coverage(extra[:, 256:384]), 0.0)
        beyond = halves(beyond)
        cb_ref[0, at, :] = col_blur([beyond, halves(first), halves(cov_ref[0, at, :])], g_ref)
        cb_ref[4, at, :] = col_blur([halves(cov_ref[1, at, :]), halves(last), beyond], g_ref)

        @pl.loop(0, 8)
        def _(s):
            d = in_chunk(c, s)
            piece_b(cb_ref, send_ref, d)

            @pl.when(d != col)
            def _():
                piece(1, d, col).start()

    own = pltpu.make_async_copy(send_ref.at[col], got_ref.at[col], own_sem)
    own.start()
    dose.wait()

    def write(c):
        lanes = pl.ds(pl.multiple_of(TILE * c, 128), TILE)
        return pltpu.make_async_copy(out_ref.at[:, lanes], out_hbm.at[:, lanes], out_sem.at[c])

    def finish(c):
        for place, tile in enumerate((1, 2, 3, 0, 4)):
            lanes = pl.ds(pl.multiple_of(TILE * c + 128 * tile, 128), 128)
            out_ref[:, lanes] = dose_ref[:, lanes] * got_ref[c, STRIPE * place : STRIPE * place + STRIPE, :]
        write(c).start()

    own.wait()
    finish(col)

    @pl.loop(1, n_col)
    def _(i):
        group = i // 8
        dz = jnp.where(group == 0, 0, jnp.where(group == 1, 2, jnp.where(group == 2, 1, 3)))
        s = lax.rem(i, 8)
        c = lax.rem(z + 4 - dz, 4) * 8 + lax.rem(y + 4 - s // 2, 4) * 2 + lax.rem(core + lax.rem(s, 2), 2)
        piece(0, c, c).wait_recv()
        piece(1, c, c).wait_recv()
        finish(c)

    @pl.when(down)
    def _():
        row_halo(0).wait_send()

    @pl.when(up)
    def _():
        row_halo(1).wait_send()

    @pl.when(right)
    def _():
        col_halo(0).wait_send()

    @pl.when(left)
    def _():
        col_halo(1).wait_send()

    @pl.loop(0, n_col)
    def _(k):
        @pl.when(k != col)
        def _():
            for part in range(2):
                piece(part, k, k).wait_send()

        write(k).wait()


def solution(mesh):
    n_row, n_col = mesh.shape["row"], mesh.shape["col"]
    any_space = pl.BlockSpec(memory_space=pl.ANY)

    def local(level_set, dose_map):
        return pl.pallas_call(
            functools.partial(tile_kernel, n_row, n_col),
            out_shape=jax.ShapeDtypeStruct(dose_map.shape, F32),
            in_specs=[any_space, any_space],
            out_specs=any_space,
            scratch_shapes=[
                pltpu.VMEM((4, PART, FINE), F32),
                pltpu.VMEM((24, FINE), F32),
                pltpu.VMEM((24, FINE), F32),
                pltpu.VMEM((TILES, PART, 128), F32),
                pltpu.VMEM((TILES, 48, 128), F32),
                pltpu.VMEM((TILES, 48, 128), F32),
                pltpu.VMEM((5, 512, 128), BF16),
                pltpu.VMEM((384, 384), BF16),
                pltpu.VMEM((2, 384, 128), BF16),
                pltpu.VMEM((TILES, CHUNK, 128), F32),
                pltpu.VMEM((2, CROWS, 128), F32),
                pltpu.VMEM((2, CROWS, 128), F32),
                pltpu.VMEM((5, CROWS, 128), F32),
                pltpu.VMEM((3, HROWS, 128), F32),
                pltpu.VMEM((2, 16, HROWS), F32),
                pltpu.VMEM((128, HROWS), F32),
                pltpu.VMEM((n_col, SLOT, 128), F32),
                pltpu.VMEM((n_col, SLOT, 128), F32),
                pltpu.VMEM(dose_map.shape, F32),
                pltpu.VMEM(dose_map.shape, F32),
                pltpu.SemaphoreType.DMA((4,)),
                pltpu.SemaphoreType.DMA((2,)),
                pltpu.SemaphoreType.DMA,
                pltpu.SemaphoreType.DMA((2,)),
                pltpu.SemaphoreType.DMA((2,)),
                pltpu.SemaphoreType.DMA((2,)),
                pltpu.SemaphoreType.DMA((2,)),
                pltpu.SemaphoreType.DMA((2, n_col)),
                pltpu.SemaphoreType.DMA((2, n_col)),
                pltpu.SemaphoreType.DMA,
                pltpu.SemaphoreType.DMA((n_col,)),
            ],
            compiler_params=pltpu.CompilerParams(
                collective_id=0, has_side_effects=True, vmem_limit_bytes=52 << 20
            ),
            name="resample_exchange",
        )(level_set, dose_map)

    return jax.shard_map(
        local,
        mesh=mesh,
        in_specs=(P("row", "col"), P(("row", "col"), None)),
        out_specs=P(("row", "col"), None),
        check_vma=False,
    )
```

time: 204 us -> 62.5 us (0.31)
  the two profiles are of different devices: /device:TPU:32 before, /device:TPU:14 now
where the time goes in v2:
time: 62.5 us; the launch traced here: 62.4 us
  Pallas kernels  61.1 us (98%)
  local copies, waits for them, and re-layouts  1.27 us (2%)
    pallas_call x1, Pallas kernels, local(): pl.pallas_call(functools.partial(tile_kernel, n_row, n_col), out_shape=ja...  61.1 us
    unnamed x1, local copies, waits for them, and re-layouts  1.27 us

profile of v2, /device:TPU:14, one launch (start us, length us, event | category | flops | bytes accessed | tf_op | source)
XLA Modules:
  0.0 62.4 jit_solution(10089588470791852868)
XLA Ops:
  0.0 61.1 %resample_exchange.1 = f32[20,20480]{1,0:T(8,128)S(1)} custom-call(f32[1600,1600]{1,0:T(8,128)} %x_hbm.1, f32[20,20480]{1,0:T(8,128)} %dose_hbm.1), custom_call_target="tpu_custom_call" | custom-call | tf_op jit(solution)/shard_map/resample_exchange/pallas_call | solution.py:438
  61.1 1.3 %copy.4 = f32[20,20480]{1,0:T(8,128)} copy(f32[20,20480]{1,0:T(8,128)S(1)} %resample_exchange.1) | data formatting | bytes 3276800

commit v3 on v2

v3 whole, which is shorter than its diff:
```python
import functools
import math

import jax
import jax.numpy as jnp
from jax import lax
from jax.experimental import pallas as pl
from jax.experimental.pallas import tpu as pltpu
from jax.sharding import PartitionSpec as P

F32, BF16 = jnp.float32, jnp.bfloat16
MESH = pl.DeviceIdType.MESH
RAW_TAPS = [math.exp(-0.5 * k * k) for k in range(5)]
TAPS = [t / (RAW_TAPS[0] + 2.0 * sum(RAW_TAPS[1:])) for t in RAW_TAPS]

FINE, TILE, STRIPE = 1600, 640, 20
TILES = 13
PART = 464
CHUNK = 176
CROWS = 656
HROWS = 768
BASES = (0, 256, 512, 896, 1152)
SLOT = 100
PART_A = 60


def to_tiles(src_ref, src_at, dst_ref, dst_at, count):
    for tile in range(TILES - 1):
        dst_ref[tile, pl.ds(dst_at, count), :] = src_ref[pl.ds(src_at, count), 128 * tile : 128 * tile + 128]
    dst_ref[12, pl.ds(dst_at, count), 0:64] = src_ref[pl.ds(src_at, count), 1536:1600]


def row_group(x_ref, tile, start, out_ref, out_row):
    a = [x_ref[tile, pl.ds(start + s, 8, stride=5), :] for s in range(-1, 6)]
    even = 3.0 * a[0] + 7.0 * a[1] + 9.0 * a[2] + 5.0 * a[3] + a[4]
    odd = a[2] + 5.0 * a[3] + 9.0 * a[4] + 7.0 * a[5] + 3.0 * a[6]
    out_ref[tile, pl.ds(out_row, 8, stride=2), :] = even
    out_ref[tile, pl.ds(out_row + 1, 8, stride=2), :] = odd


def dot(a, b):
    return jnp.dot(a, b, preferred_element_type=F32)


def tent_dot(rows, w):
    hi = rows.astype(BF16)
    rest = rows - hi.astype(F32)
    mid = rest.astype(BF16)
    low = (rest - mid.astype(F32)).astype(BF16)
    return dot(hi, w) + dot(mid, w) + dot(low, w)


def col_tile(rr_ref, count, w_ref, tile):
    first = BASES[tile] // 128
    return tent_dot(jnp.concatenate([rr_ref[first + t, 0:count, :] for t in range(4)], axis=1), w_ref[tile])


def coverage(total):
    return 1.0 / (1.0 + jnp.exp(total * (-1.0 / 1250.0)))


def halves(cover):
    hi = cover.astype(BF16)
    return hi, (cover - hi.astype(F32)).astype(BF16)


def col_blur(pieces, g_ref):
    hi = jnp.concatenate([p[0] for p in pieces], axis=1)
    low = jnp.concatenate([p[1] for p in pieces], axis=1)
    return dot(hi, g_ref[0]) + dot(low, g_ref[0]) + dot(hi, g_ref[1])


def row_blur(cb_ref, d, tile):
    first = STRIPE * d + 4
    taps = [cb_ref[tile, pl.ds(first + k, STRIPE), :] for k in range(9)]
    total = TAPS[0] * taps[4]
    for k in range(1, 5):
        total = total + TAPS[k] * (taps[4 - k] + taps[4 + k])
    return total


def piece_a(cb_ref, send_ref, d):
    for t in range(3):
        send_ref[d, STRIPE * t : STRIPE * t + STRIPE, :] = row_blur(cb_ref, d, t + 1)


def piece_b(cb_ref, send_ref, d):
    for t in range(2):
        send_ref[d, PART_A + STRIPE * t : PART_A + STRIPE * t + STRIPE, :] = row_blur(cb_ref, d, 4 * t)


def make_weights(w_ref, we_ref, g_ref):
    def tent(fine_col, coarse_col):
        return jnp.maximum(10 - jnp.abs(4 * fine_col - 10 * coarse_col - 3), 0)

    k = lax.broadcasted_iota(jnp.int32, (512, 128), 0)
    n = lax.broadcasted_iota(jnp.int32, (512, 128), 1)
    for tile in range(5):
        w_ref[tile] = tent(k + BASES[tile], n + 128 * tile).astype(F32).astype(BF16)

    k = lax.broadcasted_iota(jnp.int32, (256, 128), 0)
    n = lax.broadcasted_iota(jnp.int32, (256, 128), 1)
    to_left = tent(jnp.where(k < 128, k, k + 1408), n - 1)
    to_right = tent(jnp.where(k < 128, k, k + 1408), n + 628)
    use = jnp.logical_and(n >= 8, n < 13)
    we_ref[...] = jnp.where(n < 5, to_left, jnp.where(use, to_right, 0)).astype(F32).astype(BF16)

    k = lax.broadcasted_iota(jnp.int32, (384, 128), 0)
    n = lax.broadcasted_iota(jnp.int32, (384, 128), 1)
    off = jnp.abs(k - n - 128)
    g = jnp.zeros((384, 128), F32)
    for step in range(5):
        g = jnp.where(off == step, TAPS[step], g)
    hi, low = halves(g)
    g_ref[0] = hi
    g_ref[1] = low


def row_groups(x_ref, start, out_ref, out_row):
    for tile in range(TILES):
        row_group(x_ref, tile, start, out_ref, out_row)


def tile_kernel(
    n_row, n_col, x_hbm, dose_hbm, out_hbm,
    x_in, x_ref, end_x_ref, side_x_ref, w_ref, we_ref, g_ref, rr_ref, sum_ref, cov_ref, cb_ref,
    strip_ref, own_ref, side_ref, side_out, side_in, end_ref, end_out, end_in,
    send_ref, got_ref, dose_ref, out_ref,
    load_sem, dose_sem, row_send, row_recv, col_send, col_recv, send_sem, recv_sem, own_sem, out_sem,
):
    row, col = lax.axis_index("row"), lax.axis_index("col")
    z, y, core = col // 8, lax.rem(col // 2, 4), lax.rem(col, 2)
    up, down, left, right = row > 0, row < n_row - 1, col > 0, col < n_col - 1

    def chunk_at(step):
        return lax.rem(z + jnp.where(step == 0, 2, jnp.where(step == 1, 1, jnp.where(step == 2, 3, 0))), 4)

    def load_start(c):
        return pl.multiple_of(jnp.clip(400 * c - 24, 0, FINE - PART), 8)

    def load(c):
        return pltpu.make_async_copy(x_hbm.at[pl.ds(load_start(c), PART)], x_in.at[c], load_sem.at[c])

    for step in range(4):
        load(chunk_at(step)).start()
    dose = pltpu.make_async_copy(dose_hbm, dose_ref, dose_sem)
    dose.start()

    side_in[...] = jnp.zeros(side_in.shape, F32)
    end_in[...] = jnp.zeros(end_in.shape, F32)

    barrier = pltpu.get_barrier_semaphore()

    @pl.loop(1, n_col)
    def _(k):
        pl.semaphore_signal(barrier, 1, device_id=(row, lax.rem(col + k, n_col)), device_id_type=MESH)

    for there, other in ((up, row - 1), (down, row + 1)):
        @pl.when(there)
        def _(other=other):
            pl.semaphore_signal(barrier, 1, device_id=(other, col), device_id_type=MESH)

    make_weights(w_ref, we_ref, g_ref)
    x_ref[12, :, 64:128] = jnp.zeros((PART, 64), F32)
    end_x_ref[0, :, 0:24, :] = jnp.zeros((TILES, 24, 128), F32)
    end_x_ref[1, :, 24:48, :] = jnp.zeros((TILES, 24, 128), F32)
    end_x_ref[:, 12, :, 64:128] = jnp.zeros((2, 48, 64), F32)
    side_x_ref[:, 0:24, :] = jnp.zeros((2, 24, 128), F32)
    side_x_ref[:, FINE + 24 : FINE + 48, :] = jnp.zeros((2, 24, 128), F32)
    side_x_ref[1, 24 : FINE + 24, 64:128] = jnp.zeros((FINE, 64), F32)
    own_ref[CROWS:HROWS, :] = jnp.zeros((HROWS - CROWS, 128), F32)

    def row_halo(i):
        return pltpu.make_async_remote_copy(
            end_out.at[i], end_in.at[i],
            row_send.at[i], row_recv.at[i], device_id=(row + 1 - 2 * i, col), device_id_type=MESH)

    def col_halo(i):
        return pltpu.make_async_remote_copy(
            side_out.at[i], side_in.at[i],
            col_send.at[i], col_recv.at[i], device_id=(row, col + 1 - 2 * i), device_id_type=MESH)

    def piece(part, d, slot):
        rows = pl.ds(0, PART_A) if part == 0 else pl.ds(PART_A, SLOT - PART_A)
        return pltpu.make_async_remote_copy(
            send_ref.at[d, rows], got_ref.at[slot, rows],
            send_sem.at[part, d], recv_sem.at[part, slot], device_id=(row, d), device_id_type=MESH)

    def in_chunk(c, s):
        return 8 * c + lax.rem(y + s // 2, 4) * 2 + lax.rem(core + lax.rem(s, 2), 2)

    def resample(c):
        base = load_start(c)

        @pl.loop(0, PART // 8)
        def _(g):
            at = pl.multiple_of(8 * g, 8)
            to_tiles(x_in.at[c], at, x_ref, at, 8)

        first = jnp.clip(10 * c, 1, 29)

        @pl.loop(0, 11)
        def _(g):
            row_groups(x_ref, 40 * (first + g) - 20 - base, rr_ref, 16 * g)

        at = pl.ds(16 * first, CHUNK)
        cover = []
        for tile in range(5):
            total = col_tile(rr_ref, CHUNK, w_ref, tile)
            if tile in (0, 4):
                sum_ref[tile // 4, at, :] = total
            total = coverage(total)
            if tile in (1, 3):
                cov_ref[tile // 2, at, :] = total
            cover.append(halves(total))
        for tile in range(1, 4):
            cb_ref[tile, at, :] = col_blur(cover[tile - 1 : tile + 2], g_ref)

    def send_a(c):
        @pl.loop(0, 8)
        def _(s):
            d = in_chunk(c, s)

            @pl.when(jnp.logical_and(d > 0, d < n_col - 1))
            def _():
                piece_a(cb_ref, send_ref, d)

                @pl.when(d != col)
                def _():
                    piece(0, d, col).start()

    def sides():
        for step in range(1, 4):
            load(chunk_at(step)).wait()
        for c in range(4):
            skip = 24 if 0 < c < 3 else 64 if c == 3 else 0

            @pl.loop(0, 10)
            def _(g, c=c, skip=skip):
                source = pl.ds(pl.multiple_of(skip + 40 * g, 8), 40)
                target = pl.ds(pl.multiple_of(24 + 400 * c + 40 * g, 8), 40)
                side_x_ref[0, target, :] = x_in[c, source, 0:128]
                side_x_ref[1, target, 0:64] = x_in[c, source, 1536:1600]

        @pl.loop(0, CROWS // 16)
        def _(g):
            for side in range(2):
                row_group(side_x_ref, side, 4 + 40 * g, strip_ref, 16 * g)

        own_ref[0:CROWS, :] = tent_dot(jnp.concatenate([strip_ref[0], strip_ref[1]], axis=1), we_ref[...])
        for part in range(HROWS // 128):
            columns = jnp.transpose(own_ref[128 * part : 128 * part + 128, :])
            side_out[0, part] = columns[8:13, :]
            side_out[1, part] = columns[0:5, :]

        @pl.when(right)
        def _():
            col_halo(0).start()

        @pl.when(left)
        def _():
            col_halo(1).start()

    @pl.loop(0, 4)
    def _(step):
        c = chunk_at(step)

        @pl.when(step == 0)
        def _():
            load(c).wait()

        resample(c)

        @pl.when(step == 0)
        def _():
            pl.semaphore_wait(barrier, n_col - 1 + up.astype(jnp.int32) + down.astype(jnp.int32))

        send_a(c)

        @pl.when(step == 0)
        def _():
            sides()

    to_tiles(x_in.at[0], 0, end_x_ref.at[0], 24, 24)
    to_tiles(x_in.at[3], PART - 24, end_x_ref.at[1], 0, 24)
    for end in range(2):
        row_groups(end_x_ref.at[end], 4, rr_ref, 16 * end)
    for tile in range(5):
        end_ref[tile] = col_tile(rr_ref, 32, w_ref, tile)

    @pl.when(left)
    def _():
        col_halo(0).wait_recv()

    @pl.when(right)
    def _():
        col_halo(1).wait_recv()

    for part in range(HROWS // 128):
        held = jnp.concatenate(
            [side_in[0, part], jnp.zeros((3, 128), F32), side_in[1, part], jnp.zeros((115, 128), F32)], axis=0)
        side_ref[128 * part : 128 * part + 128, :] = jnp.transpose(held)

    def edges(at, count):
        lane = lax.broadcasted_iota(jnp.int32, (count, 128), 1)
        got, own = side_ref[at, :], own_ref[at, :]
        low, high = pltpu.roll(got, 124, 1), pltpu.roll(got, 119, 1)
        beyond = jnp.where(lane >= 124, low, jnp.where(lane < 4, high, 0.0))
        beyond = beyond + jnp.where(lane == 127, pltpu.roll(own, 127, 1), 0.0)
        beyond = beyond + jnp.where(lane == 0, pltpu.roll(own, 116, 1), 0.0)
        return jnp.where(lane == 0, low, 0.0), jnp.where(lane == 127, high, 0.0), beyond

    def held_lanes(count):
        lane = lax.broadcasted_iota(jnp.int32, (count, 128), 1)
        return jnp.logical_or(jnp.logical_and(right, lane < 4), jnp.logical_and(left, lane >= 124))

    ends = ((0, 0), (16, CROWS - 16))
    for i, i0 in ends:
        first, last, beyond = edges(pl.ds(i0, 16), 16)
        end_ref[0, i : i + 16, :] = end_ref[0, i : i + 16, :] + first
        end_ref[4, i : i + 16, :] = end_ref[4, i : i + 16, :] + last
        end_ref[5, i : i + 16, :] = beyond
    end_out[0] = end_ref[:, 20:25, :]
    end_out[1] = end_ref[:, 7:12, :]

    @pl.when(down)
    def _():
        row_halo(0).start()

    @pl.when(up)
    def _():
        row_halo(1).start()

    def send_b(d):
        piece_b(cb_ref, send_ref, d)

        @pl.when(d != col)
        def _():
            piece(1, d, col).start()

    @pl.loop(0, 4)
    def _(step):
        c = chunk_at(step)
        at = pl.ds(pl.multiple_of(16 * jnp.clip(10 * c, 1, 29), 16), CHUNK)
        first, last, beyond = edges(at, CHUNK)
        first = halves(coverage(sum_ref[0, at, :] + first))
        last = halves(coverage(sum_ref[1, at, :] + last))
        beyond = halves(jnp.where(held_lanes(CHUNK), coverage(beyond), 0.0))
        cb_ref[0, at, :] = col_blur([beyond, first, halves(cov_ref[0, at, :])], g_ref)
        cb_ref[4, at, :] = col_blur([halves(cov_ref[1, at, :]), last, beyond], g_ref)

        @pl.loop(0, 8)
        def _(s):
            d = in_chunk(c, s)

            @pl.when(jnp.logical_and(d > 0, d < n_col - 1))
            def _():
                send_b(d)

    @pl.when(up)
    def _():
        row_halo(0).wait_recv()

    @pl.when(down)
    def _():
        row_halo(1).wait_recv()

    def in_window(i0):
        j = lax.broadcasted_iota(jnp.int32, (16, 128), 0) + (TILE * row + i0 - 8)
        return jnp.logical_and(j >= 0, j < TILE * n_row)

    inside = jnp.concatenate([in_window(i0) for _, i0 in ends], axis=0)
    cover = []
    for tile in range(6):
        end_ref[tile, 4:9, :] = end_ref[tile, 4:9, :] + end_in[0, tile]
        end_ref[tile, 23:28, :] = end_ref[tile, 23:28, :] + end_in[1, tile]
        keep = inside if tile < 5 else jnp.logical_and(inside, held_lanes(32))
        cover.append(halves(jnp.where(keep, coverage(end_ref[tile]), 0.0)))
    cover = [cover[5]] + cover
    for tile in range(5):
        total = col_blur(cover[tile : tile + 3], g_ref)
        for i, i0 in ends:
            cb_ref[tile, i0 : i0 + 16, :] = total[i : i + 16]

    for d in (0, n_col - 1):
        piece_a(cb_ref, send_ref, d)

        @pl.when(col != d)
        def _(d=d):
            piece(0, d, col).start()

        send_b(d)

    own = pltpu.make_async_copy(send_ref.at[col], got_ref.at[col], own_sem)
    own.start()
    dose.wait()

    def write(c):
        lanes = pl.ds(pl.multiple_of(TILE * c, 128), TILE)
        return pltpu.make_async_copy(out_ref.at[:, lanes], out_hbm.at[:, lanes], out_sem.at[c])

    def finish(c):
        for place, tile in enumerate((1, 2, 3, 0, 4)):
            lanes = pl.ds(pl.multiple_of(TILE * c + 128 * tile, 128), 128)
            out_ref[:, lanes] = dose_ref[:, lanes] * got_ref[c, STRIPE * place : STRIPE * place + STRIPE, :]
        write(c).start()

    own.wait()
    finish(col)

    @pl.loop(1, n_col)
    def _(i):
        group = i // 8
        dz = jnp.where(group == 0, 0, jnp.where(group == 1, 2, jnp.where(group == 2, 1, 3)))
        s = lax.rem(i, 8)
        c = lax.rem(z + 4 - dz, 4) * 8 + lax.rem(y + 4 - s // 2, 4) * 2 + lax.rem(core + lax.rem(s, 2), 2)
        piece(0, c, c).wait_recv()
        piece(1, c, c).wait_recv()
        finish(c)

    @pl.when(down)
    def _():
        row_halo(0).wait_send()

    @pl.when(up)
    def _():
        row_halo(1).wait_send()

    @pl.when(right)
    def _():
        col_halo(0).wait_send()

    @pl.when(left)
    def _():
        col_halo(1).wait_send()

    @pl.loop(0, n_col)
    def _(k):
        @pl.when(k != col)
        def _():
            for part in range(2):
                piece(part, k, k).wait_send()

        write(k).wait()


def solution(mesh):
    n_row, n_col = mesh.shape["row"], mesh.shape["col"]
    any_space = pl.BlockSpec(memory_space=pl.ANY)

    def local(level_set, dose_map):
        return pl.pallas_call(
            functools.partial(tile_kernel, n_row, n_col),
            out_shape=jax.ShapeDtypeStruct(dose_map.shape, F32),
            in_specs=[any_space, any_space],
            out_specs=any_space,
            scratch_shapes=[
                pltpu.VMEM((4, PART, FINE), F32),
                pltpu.VMEM((TILES, PART, 128), F32),
                pltpu.VMEM((2, TILES, 48, 128), F32),
                pltpu.VMEM((2, FINE + 48, 128), F32),
                pltpu.VMEM((5, 512, 128), BF16),
                pltpu.VMEM((256, 128), BF16),
                pltpu.VMEM((2, 384, 128), BF16),
                pltpu.VMEM((TILES, CHUNK, 128), F32),
                pltpu.VMEM((2, CROWS, 128), F32),
                pltpu.VMEM((2, CROWS, 128), F32),
                pltpu.VMEM((5, CROWS, 128), F32),
                pltpu.VMEM((2, CROWS, 128), F32),
                pltpu.VMEM((HROWS, 128), F32),
                pltpu.VMEM((HROWS, 128), F32),
                pltpu.VMEM((2, HROWS // 128, 5, 128), F32),
                pltpu.VMEM((2, HROWS // 128, 5, 128), F32),
                pltpu.VMEM((6, 32, 128), F32),
                pltpu.VMEM((2, 6, 5, 128), F32),
                pltpu.VMEM((2, 6, 5, 128), F32),
                pltpu.VMEM((n_col, SLOT, 128), F32),
                pltpu.VMEM((n_col, SLOT, 128), F32),
                pltpu.VMEM(dose_map.shape, F32),
                pltpu.VMEM(dose_map.shape, F32),
                pltpu.SemaphoreType.DMA((4,)),
                pltpu.SemaphoreType.DMA,
                pltpu.SemaphoreType.DMA((2,)),
                pltpu.SemaphoreType.DMA((2,)),
                pltpu.SemaphoreType.DMA((2,)),
                pltpu.SemaphoreType.DMA((2,)),
                pltpu.SemaphoreType.DMA((2, n_col)),
                pltpu.SemaphoreType.DMA((2, n_col)),
                pltpu.SemaphoreType.DMA,
                pltpu.SemaphoreType.DMA((n_col,)),
            ],
            compiler_params=pltpu.CompilerParams(
                collective_id=0, has_side_effects=True, vmem_limit_bytes=52 << 20
            ),
            name="resample_exchange",
        )(level_set, dose_map)

    return jax.shard_map(
        local,
        mesh=mesh,
        in_specs=(P("row", "col"), P(("row", "col"), None)),
        out_specs=P(("row", "col"), None),
        check_vma=False,
    )
```

time: 62.5 us -> 57.2 us (0.915)
  the two profiles are of different devices: /device:TPU:14 before, /device:TPU:6 now
where the time goes in v3:
time: 57.2 us; the launch traced here: 57.1 us
  Pallas kernels  55.8 us (98%)
  local copies, waits for them, and re-layouts  1.27 us (2%)
    pallas_call x1, Pallas kernels, local(): pl.pallas_call(functools.partial(tile_kernel, n_row, n_col), out_shape=ja...  55.8 us
    unnamed x1, local copies, waits for them, and re-layouts  1.27 us

profile of v3, /device:TPU:6, one launch (start us, length us, event | category | flops | bytes accessed | tf_op | source)
XLA Modules:
  0.0 57.1 jit_solution(16244845981042364712)
XLA Ops:
  0.0 55.8 %resample_exchange.1 = f32[20,20480]{1,0:T(8,128)S(1)} custom-call(f32[1600,1600]{1,0:T(8,128)} %x_hbm.1, f32[20,20480]{1,0:T(8,128)} %dose_hbm.1), custom_call_target="tpu_custom_call" | custom-call | tf_op jit(solution)/shard_map/resample_exchange/pallas_call | solution.py:452
  55.8 1.3 %copy.4 = f32[20,20480]{1,0:T(8,128)} copy(f32[20,20480]{1,0:T(8,128)S(1)} %resample_exchange.1) | data formatting | bytes 3276800

commit v4 on v3

v4 whole, which is shorter than its diff:
```python
import functools
import math

import jax
import jax.numpy as jnp
from jax import lax
from jax.experimental import pallas as pl
from jax.experimental.pallas import tpu as pltpu
from jax.sharding import PartitionSpec as P

F32, BF16 = jnp.float32, jnp.bfloat16
MESH = pl.DeviceIdType.MESH
RAW_TAPS = [math.exp(-0.5 * k * k) for k in range(5)]
TAPS = [t / (RAW_TAPS[0] + 2.0 * sum(RAW_TAPS[1:])) for t in RAW_TAPS]

FINE, TILE, STRIPE = 1600, 640, 20
TILES = 13
PART = 264
UNIT = 96
CROWS = 656
HROWS = 768
BASES = (0, 256, 512, 896, 1152)
SLOT = 100
PART_A = 60


def to_tiles(src_ref, src_at, dst_ref, dst_at, count):
    for tile in range(TILES - 1):
        dst_ref[tile, pl.ds(dst_at, count), :] = src_ref[pl.ds(src_at, count), 128 * tile : 128 * tile + 128]
    dst_ref[12, pl.ds(dst_at, count), 0:64] = src_ref[pl.ds(src_at, count), 1536:1600]


def row_group(x_ref, tile, start, out_ref, out_row):
    a = [x_ref[tile, pl.ds(start + s, 8, stride=5), :] for s in range(-1, 6)]
    even = 3.0 * a[0] + 7.0 * a[1] + 9.0 * a[2] + 5.0 * a[3] + a[4]
    odd = a[2] + 5.0 * a[3] + 9.0 * a[4] + 7.0 * a[5] + 3.0 * a[6]
    out_ref[tile, pl.ds(out_row, 8, stride=2), :] = even
    out_ref[tile, pl.ds(out_row + 1, 8, stride=2), :] = odd


def dot(a, b):
    return jnp.dot(a, b, preferred_element_type=F32)


def tent_dot(rows, w):
    hi = rows.astype(BF16)
    rest = rows - hi.astype(F32)
    mid = rest.astype(BF16)
    low = (rest - mid.astype(F32)).astype(BF16)
    return dot(hi, w) + dot(mid, w) + dot(low, w)


def col_tile(rr_ref, count, w_ref, tile):
    first = BASES[tile] // 128
    return tent_dot(jnp.concatenate([rr_ref[first + t, 0:count, :] for t in range(4)], axis=1), w_ref[tile])


def coverage(total):
    return 1.0 / (1.0 + jnp.exp(total * (-1.0 / 1250.0)))


def halves(cover):
    hi = cover.astype(BF16)
    return hi, (cover - hi.astype(F32)).astype(BF16)


def col_blur(pieces, g_ref):
    hi = jnp.concatenate([p[0] for p in pieces], axis=1)
    low = jnp.concatenate([p[1] for p in pieces], axis=1)
    return dot(hi, g_ref[0]) + dot(low, g_ref[0]) + dot(hi, g_ref[1])


def row_blur(cb_ref, d, tile):
    first = STRIPE * d + 4
    taps = [cb_ref[tile, pl.ds(first + k, STRIPE), :] for k in range(9)]
    total = TAPS[0] * taps[4]
    for k in range(1, 5):
        total = total + TAPS[k] * (taps[4 - k] + taps[4 + k])
    return total


def piece_a(cb_ref, send_ref, d):
    for t in range(3):
        send_ref[d, STRIPE * t : STRIPE * t + STRIPE, :] = row_blur(cb_ref, d, t + 1)


def piece_b(cb_ref, send_ref, d):
    for t in range(2):
        send_ref[d, PART_A + STRIPE * t : PART_A + STRIPE * t + STRIPE, :] = row_blur(cb_ref, d, 4 * t)


def make_weights(w_ref, we_ref, g_ref):
    def tent(fine_col, coarse_col):
        return jnp.maximum(10 - jnp.abs(4 * fine_col - 10 * coarse_col - 3), 0)

    k = lax.broadcasted_iota(jnp.int32, (512, 128), 0)
    n = lax.broadcasted_iota(jnp.int32, (512, 128), 1)
    for tile in range(5):
        w_ref[tile] = tent(k + BASES[tile], n + 128 * tile).astype(F32).astype(BF16)

    k = lax.broadcasted_iota(jnp.int32, (256, 128), 0)
    n = lax.broadcasted_iota(jnp.int32, (256, 128), 1)
    to_left = tent(jnp.where(k < 128, k, k + 1408), n - 1)
    to_right = tent(jnp.where(k < 128, k, k + 1408), n + 628)
    use = jnp.logical_and(n >= 8, n < 13)
    we_ref[...] = jnp.where(n < 5, to_left, jnp.where(use, to_right, 0)).astype(F32).astype(BF16)

    k = lax.broadcasted_iota(jnp.int32, (384, 128), 0)
    n = lax.broadcasted_iota(jnp.int32, (384, 128), 1)
    off = jnp.abs(k - n - 128)
    g = jnp.zeros((384, 128), F32)
    for step in range(5):
        g = jnp.where(off == step, TAPS[step], g)
    hi, low = halves(g)
    g_ref[0] = hi
    g_ref[1] = low


def row_groups(x_ref, start, out_ref, out_row):
    for tile in range(TILES):
        row_group(x_ref, tile, start, out_ref, out_row)


def tile_kernel(
    n_row, n_col, x_hbm, dose_hbm, out_ref,
    x_in, x_ends, x_ref, end_x_ref, side_x_ref, w_ref, we_ref, g_ref, rr_ref, sum_ref, cov_ref, cb_ref,
    strip_ref, own_ref, side_ref, side_out, side_in, end_ref, end_out, end_in,
    corner_out, corner_in, send_ref, got_ref, dose_ref,
    load_sem, end_sem, dose_sem, row_send, row_recv, corner_send, corner_recv, col_send, col_recv, send_sem, recv_sem, own_sem,
):
    row, col = lax.axis_index("row"), lax.axis_index("col")
    z, y, core = col // 8, lax.rem(col // 2, 4), lax.rem(col, 2)
    up, down, left, right = row > 0, row < n_row - 1, col > 0, col < n_col - 1

    def pick(step, values):
        out = values[0]
        for k, value in enumerate(values[1:], 1):
            out = jnp.where(step == k, value, out)
        return out

    def unit_at(step):
        c = lax.rem(z + pick(step, (2, 2, 1, 3, 1, 3, 0, 0)), 4)
        return 2 * c + lax.rem(y // 2 + pick(step, (0, 1, 0, 0, 1, 1, 0, 1)), 2)

    def load_start(u):
        return pl.multiple_of(jnp.clip(200 * u - 24, 0, FINE - PART), 8)

    def load(u):
        return pltpu.make_async_copy(x_hbm.at[pl.ds(load_start(u), PART)], x_in.at[u], load_sem.at[u])

    end_loads = [
        pltpu.make_async_copy(x_hbm.at[pl.ds(at, 24)], x_ends.at[i], end_sem.at[i]) for i, at in enumerate((0, FINE - 24))
    ]
    for end_load in end_loads:
        end_load.start()
    for step in range(8):
        load(unit_at(step)).start()
    dose = pltpu.make_async_copy(dose_hbm, dose_ref, dose_sem)
    dose.start()

    side_in[...] = jnp.zeros(side_in.shape, F32)
    end_in[...] = jnp.zeros(end_in.shape, F32)
    corner_in[...] = jnp.zeros(corner_in.shape, F32)

    barrier = pltpu.get_barrier_semaphore()

    @pl.loop(1, n_col)
    def _(k):
        pl.semaphore_signal(barrier, 1, device_id=(row, lax.rem(col + k, n_col)), device_id_type=MESH)

    around = [
        (jnp.logical_and(dv, dh) if dh is not None else dv, row + v, col + h)
        for dv, v in ((up, -1), (down, 1))
        for dh, h in ((None, 0), (left, -1), (right, 1))
    ]
    for there, other_row, other_col in around:
        @pl.when(there)
        def _(other_row=other_row, other_col=other_col):
            pl.semaphore_signal(barrier, 1, device_id=(other_row, other_col), device_id_type=MESH)

    make_weights(w_ref, we_ref, g_ref)
    x_ref[12, :, 64:128] = jnp.zeros((PART, 64), F32)
    end_x_ref[0, :, 0:24, :] = jnp.zeros((TILES, 24, 128), F32)
    end_x_ref[1, :, 24:48, :] = jnp.zeros((TILES, 24, 128), F32)
    end_x_ref[:, 12, :, 64:128] = jnp.zeros((2, 48, 64), F32)
    side_x_ref[:, 0:24, :] = jnp.zeros((2, 24, 128), F32)
    side_x_ref[:, FINE + 24 : FINE + 48, :] = jnp.zeros((2, 24, 128), F32)
    side_x_ref[1, 24 : FINE + 24, 64:128] = jnp.zeros((FINE, 64), F32)
    own_ref[CROWS:HROWS, :] = jnp.zeros((HROWS - CROWS, 128), F32)

    def row_halo(i):
        return pltpu.make_async_remote_copy(
            end_out.at[i], end_in.at[i],
            row_send.at[i], row_recv.at[i], device_id=(row + 1 - 2 * i, col), device_id_type=MESH)

    corners = [(v, h, jnp.logical_and(dv, dh)) for v, dv in ((0, down), (1, up)) for h, dh in ((0, right), (1, left))]
    corners_in = [(v, h, jnp.logical_and(dv, dh)) for v, dv in ((0, up), (1, down)) for h, dh in ((0, left), (1, right))]

    def corner(v, h):
        return pltpu.make_async_remote_copy(
            corner_out.at[v], corner_in.at[v, h],
            corner_send.at[v, h], corner_recv.at[v, h],
            device_id=(row + 1 - 2 * v, col + 1 - 2 * h), device_id_type=MESH)

    def col_halo(i):
        return pltpu.make_async_remote_copy(
            side_out.at[i], side_in.at[i],
            col_send.at[i], col_recv.at[i], device_id=(row, col + 1 - 2 * i), device_id_type=MESH)

    def piece(part, d, slot):
        rows = pl.ds(0, PART_A) if part == 0 else pl.ds(PART_A, SLOT - PART_A)
        return pltpu.make_async_remote_copy(
            send_ref.at[d, rows], got_ref.at[slot, rows],
            send_sem.at[part], recv_sem.at[slot], device_id=(row, d), device_id_type=MESH)

    def stripe(u, s):
        return 4 * u + lax.rem(y + s // 2, 2) * 2 + lax.rem(core + lax.rem(s, 2), 2)

    def first_row(u):
        return pl.multiple_of(16 * jnp.clip(5 * u, 1, 34), 16)

    def resample(u):
        base = load_start(u)

        @pl.loop(0, PART // 24)
        def _(g):
            at = pl.multiple_of(24 * g, 8)
            to_tiles(x_in.at[u], at, x_ref, at, 24)

        first = first_row(u)

        @pl.loop(0, UNIT // 16)
        def _(g):
            row_groups(x_ref, 40 * (first // 16 + g) - 20 - base, rr_ref, 16 * g)

        at = pl.ds(first, UNIT)
        cover = []
        for tile in range(5):
            total = col_tile(rr_ref, UNIT, w_ref, tile)
            if tile in (0, 4):
                sum_ref[tile // 4, at, :] = total
            total = coverage(total)
            if tile in (1, 3):
                cov_ref[tile // 2, at, :] = total
            cover.append(halves(total))
        for tile in range(1, 4):
            cb_ref[tile, at, :] = col_blur(cover[tile - 1 : tile + 2], g_ref)

    def send_a(u, end):
        @pl.loop(0, 4)
        def _(s):
            d = stripe(u, s)
            is_end = jnp.logical_or(d == 0, d == n_col - 1)

            @pl.when(is_end == end)
            def _():
                piece_a(cb_ref, send_ref, d)

                @pl.when(d != col)
                def _():
                    piece(0, d, col).start()

            if end:
                piece_b(cb_ref, send_ref, d)

                @pl.when(d != col)
                def _():
                    piece(1, d, col).start()

    def lanes_of(count):
        return lax.broadcasted_iota(jnp.int32, (count, 128), 1)

    def beyond_own(own):
        lane = lanes_of(own.shape[0])
        return jnp.where(lane == 127, pltpu.roll(own, 127, 1), jnp.where(lane == 0, pltpu.roll(own, 116, 1), 0.0))

    def ends_own():
        for i in range(2):
            end_loads[i].wait()
            to_tiles(x_ends.at[i], 0, end_x_ref.at[i], 24 - 24 * i, 24)
            row_groups(end_x_ref.at[i], 4, rr_ref, 16 * i)
        for tile in range(5):
            end_ref[tile] = col_tile(rr_ref, 32, w_ref, tile)
        own = tent_dot(jnp.concatenate([rr_ref[0, 0:32, :], rr_ref[12, 0:32, :]], axis=1), we_ref[...])
        end_ref[5] = beyond_own(own)
        end_out[0] = end_ref[:, 20:25, :]
        end_out[1] = end_ref[:, 7:12, :]
        corner_out[0] = own[20:25]
        corner_out[1] = own[7:12]

    def send_ends():
        @pl.when(down)
        def _():
            row_halo(0).start()

        @pl.when(up)
        def _():
            row_halo(1).start()

        for v, h, there in corners:
            @pl.when(there)
            def _(v=v, h=h):
                corner(v, h).start()

    def sides():
        for step in range(1, 8):
            load(unit_at(step)).wait()

        @pl.loop(0, 8)
        def _(u):
            for g in range(5):
                source = pl.ds(pl.multiple_of(200 * u - load_start(u) + 40 * g, 8), 40)
                target = pl.ds(pl.multiple_of(24 + 200 * u + 40 * g, 8), 40)
                side_x_ref[0, target, :] = x_in[u, source, 0:128]
                side_x_ref[1, target, 0:64] = x_in[u, source, 1536:1600]

        @pl.loop(0, CROWS // 16)
        def _(g):
            for side in range(2):
                row_group(side_x_ref, side, 4 + 40 * g, strip_ref, 16 * g)

        own_ref[0:CROWS, :] = tent_dot(jnp.concatenate([strip_ref[0], strip_ref[1]], axis=1), we_ref[...])
        for part in range(HROWS // 128):
            columns = jnp.transpose(own_ref[128 * part : 128 * part + 128, :])
            side_out[0, part] = columns[8:13, :]
            side_out[1, part] = columns[0:5, :]

        @pl.when(right)
        def _():
            col_halo(0).start()

        @pl.when(left)
        def _():
            col_halo(1).start()

    ends = ((0, 0), (16, CROWS - 16))

    def in_window(i0):
        j = lax.broadcasted_iota(jnp.int32, (16, 128), 0) + (TILE * row + i0 - 8)
        return jnp.logical_and(j >= 0, j < TILE * n_row)

    def ends_a():
        @pl.when(up)
        def _():
            row_halo(0).wait_recv()

        @pl.when(down)
        def _():
            row_halo(1).wait_recv()

        inside = jnp.concatenate([in_window(i0) for _, i0 in ends], axis=0)
        cover = []
        for tile in range(6):
            end_ref[tile, 4:9, :] = end_ref[tile, 4:9, :] + end_in[0, tile]
            end_ref[tile, 23:28, :] = end_ref[tile, 23:28, :] + end_in[1, tile]
            if tile < 5:
                cover.append(halves(jnp.where(inside, coverage(end_ref[tile]), 0.0)))
        for tile in range(1, 4):
            total = col_blur(cover[tile - 1 : tile + 2], g_ref)
            for i, i0 in ends:
                cb_ref[tile, i0 : i0 + 16, :] = total[i : i + 16]

    ends_own()

    @pl.loop(0, 8)
    def _(step):
        u = unit_at(step)

        @pl.when(step == 0)
        def _():
            load(u).wait()

        resample(u)

        @pl.when(step == 0)
        def _():
            near = n_col - 1
            for there, _, _ in around:
                near = near + there.astype(jnp.int32)
            pl.semaphore_wait(barrier, near)
            send_ends()

        send_a(u, False)

        @pl.when(step == 0)
        def _():
            sides()

    ends_a()

    @pl.when(left)
    def _():
        col_halo(0).wait_recv()

    @pl.when(right)
    def _():
        col_halo(1).wait_recv()

    for part in range(HROWS // 128):
        held = jnp.concatenate(
            [side_in[0, part], jnp.zeros((3, 128), F32), side_in[1, part], jnp.zeros((115, 128), F32)], axis=0)
        side_ref[128 * part : 128 * part + 128, :] = jnp.transpose(held)

    def edges(at, count):
        lane, got = lanes_of(count), side_ref[at, :]
        low, high = pltpu.roll(got, 124, 1), pltpu.roll(got, 119, 1)
        beyond = jnp.where(lane >= 124, low, jnp.where(lane < 4, high, 0.0))
        return jnp.where(lane == 0, low, 0.0), jnp.where(lane == 127, high, 0.0), beyond

    def held_lanes(count):
        lane = lanes_of(count)
        return jnp.logical_or(jnp.logical_and(right, lane < 4), jnp.logical_and(left, lane >= 124))

    def blur_sides(at, count, first, last, beyond):
        first, last = halves(first), halves(last)
        beyond = halves(jnp.where(held_lanes(count), beyond, 0.0))
        return (
            col_blur([beyond, first, halves(cov_ref[0, at, :])], g_ref),
            col_blur([halves(cov_ref[1, at, :]), last, beyond], g_ref),
        )

    for v, h, there in corners_in:
        @pl.when(there)
        def _(v=v, h=h):
            corner(v, h).wait_recv()

    lane = lanes_of(5)
    for v, (i, i0) in enumerate(ends):
        first, last, beyond = edges(pl.ds(i0, 16), 16)
        end_ref[0, i : i + 16, :] = end_ref[0, i : i + 16, :] + first
        end_ref[4, i : i + 16, :] = end_ref[4, i : i + 16, :] + last
        end_ref[5, i : i + 16, :] = end_ref[5, i : i + 16, :] + beyond
        low, high = pltpu.roll(corner_in[v, 0], 116, 1), pltpu.roll(corner_in[v, 1], 127, 1)
        rows = slice(4, 9) if v == 0 else slice(23, 28)
        end_ref[0, rows, :] = end_ref[0, rows, :] + jnp.where(lane == 0, low, 0.0)
        end_ref[4, rows, :] = end_ref[4, rows, :] + jnp.where(lane == 127, high, 0.0)
        end_ref[5, rows, :] = end_ref[5, rows, :] + jnp.where(lane >= 124, low, jnp.where(lane < 4, high, 0.0))

    for i, i0 in ends:
        inside = in_window(i0)
        at, part = pl.ds(i0, 16), slice(i, i + 16)
        for k, tile in ((0, 1), (1, 3)):
            cov_ref[k, at, :] = jnp.where(inside, coverage(end_ref[tile, part, :]), 0.0)
        first, last, beyond = (jnp.where(inside, coverage(end_ref[tile, part, :]), 0.0) for tile in (0, 4, 5))
        cb_ref[0, at, :], cb_ref[4, at, :] = blur_sides(at, 16, first, last, beyond)

    @pl.loop(0, 8)
    def _(step):
        u = unit_at(step)
        at = pl.ds(first_row(u), UNIT)
        first, last, beyond = edges(at, UNIT)
        first = coverage(sum_ref[0, at, :] + first)
        last = coverage(sum_ref[1, at, :] + last)
        beyond = coverage(beyond + beyond_own(own_ref[at, :]))
        cb_ref[0, at, :], cb_ref[4, at, :] = blur_sides(at, UNIT, first, last, beyond)

        send_a(u, True)

    own = pltpu.make_async_copy(send_ref.at[col], got_ref.at[col], own_sem)
    own.start()
    dose.wait()

    def finish(c):
        for place, tile in enumerate((1, 2, 3, 0, 4)):
            lanes = pl.ds(pl.multiple_of(TILE * c + 128 * tile, 128), 128)
            out_ref[:, lanes] = dose_ref[:, lanes] * got_ref[c, STRIPE * place : STRIPE * place + STRIPE, :]

    own.wait()

    @pl.loop(0, 4)
    def _(i):
        dz = jnp.where(i == 0, 0, jnp.where(i == 1, 2, jnp.where(i == 2, 1, 3)))
        group = lax.rem(z + 4 - dz, 4)

        @pl.loop(0, 8)
        def _(s):
            c = group * 8 + lax.rem(y + 4 - s // 2, 4) * 2 + lax.rem(core + lax.rem(s, 2), 2)

            @pl.when(c != col)
            def _():
                pltpu.make_async_copy(send_ref.at[c], got_ref.at[c], recv_sem.at[c]).wait()

            finish(c)

    @pl.when(down)
    def _():
        row_halo(0).wait_send()

    @pl.when(up)
    def _():
        row_halo(1).wait_send()

    for v, h, there in corners:
        @pl.when(there)
        def _(v=v, h=h):
            corner(v, h).wait_send()

    @pl.when(right)
    def _():
        col_halo(0).wait_send()

    @pl.when(left)
    def _():
        col_halo(1).wait_send()

    for part, rows in enumerate((PART_A, SLOT - PART_A)):
        sent = send_ref.at[pl.ds(0, n_col - 1), pl.ds(0, rows)]
        pltpu.make_async_copy(sent, sent, send_sem.at[part]).wait()


def solution(mesh):
    n_row, n_col = mesh.shape["row"], mesh.shape["col"]
    any_space = pl.BlockSpec(memory_space=pl.ANY)

    def local(level_set, dose_map):
        return pl.pallas_call(
            functools.partial(tile_kernel, n_row, n_col),
            out_shape=jax.ShapeDtypeStruct(dose_map.shape, F32),
            in_specs=[any_space, any_space],
            out_specs=pl.BlockSpec(memory_space=pltpu.VMEM),
            scratch_shapes=[
                pltpu.VMEM((8, PART, FINE), F32),
                pltpu.VMEM((2, 24, FINE), F32),
                pltpu.VMEM((TILES, PART, 128), F32),
                pltpu.VMEM((2, TILES, 48, 128), F32),
                pltpu.VMEM((2, FINE + 48, 128), F32),
                pltpu.VMEM((5, 512, 128), BF16),
                pltpu.VMEM((256, 128), BF16),
                pltpu.VMEM((2, 384, 128), BF16),
                pltpu.VMEM((TILES, UNIT, 128), F32),
                pltpu.VMEM((2, CROWS, 128), F32),
                pltpu.VMEM((2, CROWS, 128), F32),
                pltpu.VMEM((5, CROWS, 128), F32),
                pltpu.VMEM((2, CROWS, 128), F32),
                pltpu.VMEM((HROWS, 128), F32),
                pltpu.VMEM((HROWS, 128), F32),
                pltpu.VMEM((2, HROWS // 128, 5, 128), F32),
                pltpu.VMEM((2, HROWS // 128, 5, 128), F32),
                pltpu.VMEM((6, 32, 128), F32),
                pltpu.VMEM((2, 6, 5, 128), F32),
                pltpu.VMEM((2, 6, 5, 128), F32),
                pltpu.VMEM((2, 5, 128), F32),
                pltpu.VMEM((2, 2, 5, 128), F32),
                pltpu.VMEM((n_col, SLOT, 128), F32),
                pltpu.VMEM((n_col, SLOT, 128), F32),
                pltpu.VMEM(dose_map.shape, F32),
                pltpu.SemaphoreType.DMA((8,)),
                pltpu.SemaphoreType.DMA((2,)),
                pltpu.SemaphoreType.DMA,
                pltpu.SemaphoreType.DMA((2,)),
                pltpu.SemaphoreType.DMA((2,)),
                pltpu.SemaphoreType.DMA((2, 2)),
                pltpu.SemaphoreType.DMA((2, 2)),
                pltpu.SemaphoreType.DMA((2,)),
                pltpu.SemaphoreType.DMA((2,)),
                pltpu.SemaphoreType.DMA((2,)),
                pltpu.SemaphoreType.DMA((n_col,)),
                pltpu.SemaphoreType.DMA,
            ],
            compiler_params=pltpu.CompilerParams(
                collective_id=0, has_side_effects=True, vmem_limit_bytes=52 << 20
            ),
            name="resample_exchange",
        )(level_set, dose_map)

    return jax.shard_map(
        local,
        mesh=mesh,
        in_specs=(P("row", "col"), P(("row", "col"), None)),
        out_specs=P(("row", "col"), None),
        check_vma=False,
    )
```

time: 57.2 us -> 55.4 us (0.969)
  the two profiles are of different devices: /device:TPU:6 before, /device:TPU:1 now
where the time goes in v4:
time: 55.4 us; the launch traced here: 55.3 us
  Pallas kernels  54 us (97%)
  local copies, waits for them, and re-layouts  1.27 us (2%)
    pallas_call x1, Pallas kernels, local(): pl.pallas_call(functools.partial(tile_kernel, n_row, n_col), out_shape=ja...  54 us
    unnamed x1, local copies, waits for them, and re-layouts  1.27 us

profile of v4, /device:TPU:1, one launch (start us, length us, event | category | flops | bytes accessed | tf_op | source)
XLA Modules:
  0.0 55.3 jit_solution(807894748388112454)
XLA Ops:
  0.0 54.0 %resample_exchange.1 = f32[20,20480]{1,0:T(8,128)S(1)} custom-call(f32[1600,1600]{1,0:T(8,128)} %x_hbm.1, f32[20,20480]{1,0:T(8,128)} %dose_hbm.1), custom_call_target="tpu_custom_call" | custom-call | tf_op jit(solution)/shard_map/resample_exchange/pallas_call | solution.py:516
  54.1 1.3 %copy.4 = f32[20,20480]{1,0:T(8,128)} copy(f32[20,20480]{1,0:T(8,128)S(1)} %resample_exchange.1) | data formatting | bytes 3276800

commit v5 on v4

--- a/solution.py
+++ b/solution.py
@@ -153,10 +153,7 @@
     ]
     for end_load in end_loads:
         end_load.start()
-    for step in range(8):
-        load(unit_at(step)).start()
-    dose = pltpu.make_async_copy(dose_hbm, dose_ref, dose_sem)
-    dose.start()
+    load(unit_at(0)).start()
 
     side_in[...] = jnp.zeros(side_in.shape, F32)
     end_in[...] = jnp.zeros(end_in.shape, F32)
@@ -178,6 +175,10 @@
         def _(other_row=other_row, other_col=other_col):
             pl.semaphore_signal(barrier, 1, device_id=(other_row, other_col), device_id_type=MESH)
 
+    for step in range(1, 8):
+        load(unit_at(step)).start()
+    dose = pltpu.make_async_copy(dose_hbm, dose_ref, dose_sem)
+    dose.start()
     make_weights(w_ref, we_ref, g_ref)
     x_ref[12, :, 64:128] = jnp.zeros((PART, 64), F32)
     end_x_ref[0, :, 0:24, :] = jnp.zeros((TILES, 24, 128), F32)
@@ -211,7 +212,7 @@
         rows = pl.ds(0, PART_A) if part == 0 else pl.ds(PART_A, SLOT - PART_A)
         return pltpu.make_async_remote_copy(
             send_ref.at[d, rows], got_ref.at[slot, rows],
-            send_sem.at[part], recv_sem.at[slot], device_id=(row, d), device_id_type=MESH)
+            send_sem.at[part], recv_sem.at[slot // 8], device_id=(row, d), device_id_type=MESH)
 
     def stripe(u, s):
         return 4 * u + lax.rem(y + s // 2, 2) * 2 + lax.rem(core + lax.rem(s, 2), 2)
@@ -467,20 +468,20 @@
 
     own.wait()
 
-    @pl.loop(0, 4)
-    def _(i):
-        dz = jnp.where(i == 0, 0, jnp.where(i == 1, 2, jnp.where(i == 2, 1, 3)))
-        group = lax.rem(z + 4 - dz, 4)
-
-        @pl.loop(0, 8)
-        def _(s):
-            c = group * 8 + lax.rem(y + 4 - s // 2, 4) * 2 + lax.rem(core + lax.rem(s, 2), 2)
-
-            @pl.when(c != col)
-            def _():
-                pltpu.make_async_copy(send_ref.at[c], got_ref.at[c], recv_sem.at[c]).wait()
-
-            finish(c)
+    def received(group, count):
+        got = got_ref.at[pl.ds(0, count)]
+        pltpu.make_async_copy(got, got, recv_sem.at[group]).wait()
+
+    received(z, 7)
+    for s in range(8):
+        finish(8 * z + s)
+
+    @pl.loop(1, 4)
+    def _(dz):
+        group = lax.rem(z + dz, 4)
+        received(group, 8)
+        for s in range(8):
+            finish(8 * group + s)
 
     @pl.when(down)
     def _():
@@ -554,7 +555,7 @@
                 pltpu.SemaphoreType.DMA((2,)),
                 pltpu.SemaphoreType.DMA((2,)),
                 pltpu.SemaphoreType.DMA((2,)),
-                pltpu.SemaphoreType.DMA((n_col,)),
+                pltpu.SemaphoreType.DMA((4,)),
                 pltpu.SemaphoreType.DMA,
             ],
             compiler_params=pltpu.CompilerParams(

time: 55.4 us -> 53.5 us (0.966)
  Pallas kernels: 54 us -> 52.2 us
    pallas_call x1, Pallas kernels: 54 us -> 52.2 us  [local(): pl.pallas_call(functools.partial(tile_kernel, n_row, n_col), out_shape=ja...]
where the time goes in v5:
time: 53.5 us; the launch traced here: 53.4 us
  Pallas kernels  52.2 us (98%)
  local copies, waits for them, and re-layouts  1.27 us (2%)
    pallas_call x1, Pallas kernels, local(): pl.pallas_call(functools.partial(tile_kernel, n_row, n_col), out_shape=ja...  52.2 us
    unnamed x1, local copies, waits for them, and re-layouts  1.27 us

profile of v5, /device:TPU:1, one launch (start us, length us, event | category | flops | bytes accessed | tf_op | source)
XLA Modules:
  0.0 53.4 jit_solution(18337181414854923741)
XLA Ops:
  0.0 52.2 %resample_exchange.1 = f32[20,20480]{1,0:T(8,128)S(1)} custom-call(f32[1600,1600]{1,0:T(8,128)} %x_hbm.1, f32[20,20480]{1,0:T(8,128)} %dose_hbm.1), custom_call_target="tpu_custom_call" | custom-call | tf_op jit(solution)/shard_map/resample_exchange/pallas_call | solution.py:517
  52.2 1.3 %copy.4 = f32[20,20480]{1,0:T(8,128)} copy(f32[20,20480]{1,0:T(8,128)S(1)} %resample_exchange.1) | data formatting | bytes 3276800

commit v6 on v5

--- a/solution.py
+++ b/solution.py
@@ -161,7 +161,7 @@
 
     barrier = pltpu.get_barrier_semaphore()
 
-    @pl.loop(1, n_col)
+    @pl.loop(1, n_col, unroll=True)
     def _(k):
         pl.semaphore_signal(barrier, 1, device_id=(row, lax.rem(col + k, n_col)), device_id_type=MESH)
 

time: 53.5 us -> 53.4 us (level)
  no operation moved by 1% of the time
where the time goes in v6:
time: 53.4 us
  Pallas kernels  52.1 us (98%)
  local copies, waits for them, and re-layouts  1.27 us (2%)
    pallas_call x1, Pallas kernels, local(): pl.pallas_call(functools.partial(tile_kernel, n_row, n_col), out_shape=ja...  52.1 us
    unnamed x1, local copies, waits for them, and re-layouts  1.27 us

profile of v6, /device:TPU:1, one launch (start us, length us, event | category | flops | bytes accessed | tf_op | source)
XLA Modules:
  0.0 53.4 jit_solution(1979466022817940904)
XLA Ops:
  0.0 52.1 %resample_exchange.1 = f32[20,20480]{1,0:T(8,128)S(1)} custom-call(f32[1600,1600]{1,0:T(8,128)} %x_hbm.1, f32[20,20480]{1,0:T(8,128)} %dose_hbm.1), custom_call_target="tpu_custom_call" | custom-call | tf_op jit(solution)/shard_map/resample_exchange/pallas_call | solution.py:517
  52.1 1.3 %copy.4 = f32[20,20480]{1,0:T(8,128)} copy(f32[20,20480]{1,0:T(8,128)S(1)} %resample_exchange.1) | data formatting | bytes 3276800
